TPU v7x, 32 devices: a whole 2x2x4 slice. The times are simulated.
32 devices in a mesh: ccd: 4 (over y, core), strip: 8 (over z, x).
Axes of the slice: x: 2, y: 2, z: 4, core: 2. Of those that a mesh axis runs over, the one named last changes fastest.
Arguments:
- tile_store: float32 [576, 16, 128], P(('ccd', 'strip')), may hold values from -13 to 13
- tile_source: int32 [32, 18], replicated, may hold values from 0 to 31, as said below
- tile_slot: int32 [32, 18], replicated, may hold values from 0 to 17, as said below
- shift_cols: int32 [4], P('ccd'), may hold values from -117 to 117
- spatial_order: int32 [4], P('ccd'), may hold values from 0 to 2
- science: float32 [512, 2048], P(('ccd', 'strip')), may hold values from -16 to 16
Outputs:
- difference: float32 [512, 2048], P(('ccd', 'strip'))
Inputs may be any that keep to these rules, and one draw needn't show every extreme that they name: `tile_source`: every device holds exactly 18 tiles over all strips, one device holds at most 1 tiles of one strip, and some device holds exactly 1 tiles of some strip. `tile_slot`: each position of each store is named by exactly one pair of strip and tile.
All inputs are finite; a program needn't handle non-finite values.
Results may differ from a plain program's by a relative error of at most 0.005.
Values sent between devices are 32-bit elements; how exact they have to be, the bound alone decides.
No kernel may reach another device: no remote copies, remote signals or barrier semaphores. Data moves between devices by JAX's collectives and lax.ppermute only.
A program may use at most 64 MiB of HBM per device.

v0:
```python
import jax
import jax.numpy as jnp
from jax import lax
from jax.sharding import PartitionSpec as P

H = 11
CM = 128
RB = 4
NB = 27
NSP = 6
TW = 2304


gauss_sigmas = (0.7, 1.5, 3.0)
poly_degrees = (4, 2, 2)
mono_degrees = (0, 1, 1, 2, 2, 2)
ridge_weight = 0.05


def with_halo(cells, sides, width):
    for axis, dim in sides:
        count = lax.axis_size(axis)
        ends = count - 1
        head = lax.slice_in_dim(cells, 0, width, axis=dim)
        tail = lax.slice_in_dim(cells, cells.shape[dim] - width, cells.shape[dim], axis=dim)
        cells = jnp.concatenate(
            [
                lax.ppermute(tail, axis, [(i, (i + 1) % count) for i in range(ends)]),
                cells,
                lax.ppermute(head, axis, [((i + 1) % count, i) for i in range(ends)]),
            ],
            axis=dim,
        )
    return cells


def tap_table(half_width):
    offsets = jnp.arange(-half_width, half_width + 1).astype(jnp.float32)
    table_rows = []
    for sigma_value, top_degree in zip(gauss_sigmas, poly_degrees):
        envelope = jnp.exp(-offsets * offsets / (2.0 * sigma_value * sigma_value))
        envelope_sum = jnp.sum(envelope)
        for power_of in range(top_degree + 1):
            table_rows.append(envelope * (offsets / sigma_value) ** power_of / envelope_sum)
    return jnp.stack(table_rows)


def band_tables(tap_rows, half_width, block_rows):
    tap_count = 2 * half_width + 1
    out_pos = jnp.arange(block_rows)[:, None]
    in_pos = jnp.arange(block_rows + 2 * half_width)[None, :]
    onehot = ((in_pos - out_pos)[:, :, None] == jnp.arange(tap_count)[None, None, :]).astype(
        jnp.float32
    )
    band_rows = []
    first_row = 0
    for top_degree in poly_degrees:
        group_taps = tap_rows[first_row : first_row + top_degree + 1]
        band_rows.append(
            jnp.einsum("rka,ja->jrk", onehot, group_taps, precision=lax.Precision.HIGHEST).astype(
                jnp.bfloat16
            )
        )
        first_row += top_degree + 1
    return band_rows


def horizontal_pass(window, tap_rows, out_cols):
    outputs = []
    tap_count = tap_rows.shape[1]
    for filter_id in range(tap_rows.shape[0]):
        taps_now = tap_rows[filter_id]

        def add_tap(tap_id, running, taps_now=taps_now):
            return running + taps_now[tap_id] * lax.dynamic_slice_in_dim(
                window, tap_id, out_cols, 1
            )

        summed = lax.fori_loop(
            0, tap_count, add_tap, jnp.zeros((window.shape[0], out_cols), jnp.float32)
        )
        outputs.append(summed.astype(jnp.bfloat16))
    groups = []
    first_row = 0
    for top_degree in poly_degrees:
        groups.append(jnp.stack(outputs[first_row : first_row + top_degree + 1]))
        first_row += top_degree + 1
    return groups


def block_basis(groups, band_rows, start_row, block_rows, half_width):
    pieces = []
    for group_id, top_degree in enumerate(poly_degrees):
        rows_in = lax.dynamic_slice_in_dim(
            groups[group_id], start_row, block_rows + 2 * half_width, 1
        )
        mixed = jnp.einsum(
            "jrk,ikx->ijrx", band_rows[group_id], rows_in, preferred_element_type=jnp.float32
        ).astype(jnp.bfloat16)
        for horiz_degree in range(top_degree + 1):
            pieces.append(mixed[horiz_degree, : top_degree + 1 - horiz_degree])
    return jnp.concatenate(pieces, axis=0)


def monomials(first_row, block_rows, total_rows, col_count):
    row_pos = (first_row + jnp.arange(block_rows)).astype(jnp.float32)
    vertical_pos = 2.0 * (row_pos + 0.5) / total_rows - 1.0
    horizontal_pos = 2.0 * (jnp.arange(col_count).astype(jnp.float32) + 0.5) / col_count - 1.0
    vertical_grid = jnp.broadcast_to(vertical_pos[:, None], (block_rows, col_count))
    horizontal_grid = jnp.broadcast_to(horizontal_pos[None, :], (block_rows, col_count))
    ones_grid = jnp.ones((block_rows, col_count), jnp.float32)
    return jnp.stack(
        [
            ones_grid,
            horizontal_grid,
            vertical_grid,
            horizontal_grid * horizontal_grid,
            horizontal_grid * vertical_grid,
            vertical_grid * vertical_grid,
        ]
    )


def design_rows(basis_block, mono_grid):
    kernel_part = (basis_block.astype(jnp.float32)[:, None] * mono_grid[None]).astype(jnp.bfloat16)
    kernel_part = kernel_part.reshape(basis_block.shape[0] * mono_grid.shape[0], -1)
    back_part = mono_grid.astype(jnp.bfloat16).reshape(mono_grid.shape[0], -1)
    return jnp.concatenate([kernel_part, back_part], axis=0)


def forward_solve(lower, values):
    count = values.shape[0]

    def step_down(row_id, known):
        row_now = lax.dynamic_index_in_dim(lower, row_id, 0, keepdims=False)
        partial_value = jnp.sum(row_now * known)
        value_now = (
            lax.dynamic_index_in_dim(values, row_id, 0, keepdims=False) - partial_value
        ) / row_now[row_id]
        return lax.dynamic_update_index_in_dim(known, value_now, row_id, 0)

    return lax.fori_loop(0, count, step_down, jnp.zeros((count,), jnp.float32))


def backward_solve(lower, values):
    count = values.shape[0]

    def step_up(step_id, known):
        row_id = count - 1 - step_id
        column_now = lax.dynamic_index_in_dim(lower, row_id, 1, keepdims=False)
        partial_value = jnp.sum(column_now * known)
        value_now = (
            lax.dynamic_index_in_dim(values, row_id, 0, keepdims=False) - partial_value
        ) / column_now[row_id]
        return lax.dynamic_update_index_in_dim(known, value_now, row_id, 0)

    return lax.fori_loop(0, count, step_up, jnp.zeros((count,), jnp.float32))


def solve_kernel(gram_total, rhs_total, order_value, basis_count):
    degree_list = jnp.array(mono_degrees, dtype=jnp.int32)
    kernel_on = (degree_list <= order_value).astype(jnp.float32)
    active = jnp.concatenate(
        [jnp.tile(kernel_on, basis_count), jnp.ones((len(mono_degrees),), jnp.float32)]
    )
    masked = gram_total * active[:, None] * active[None, :] + jnp.diag(1.0 - active)
    system = masked + ridge_weight * jnp.diag(jnp.diag(masked))
    lower = jnp.linalg.cholesky(system)
    middle = forward_solve(lower, rhs_total * active)
    return backward_solve(lower, middle)


def block_difference(basis_block, mono_grid, coeffs, science_block, basis_count):
    spatial_count = mono_grid.shape[0]
    kernel_coef = coeffs[: basis_count * spatial_count].reshape(basis_count, spatial_count)
    back_coef = coeffs[basis_count * spatial_count :]
    weights = jnp.zeros((basis_count,) + mono_grid.shape[1:], jnp.float32)
    background = jnp.zeros(mono_grid.shape[1:], jnp.float32)
    for mono_id in range(spatial_count):
        weights = weights + kernel_coef[:, mono_id, None, None] * mono_grid[mono_id][None]
        background = background + back_coef[mono_id] * mono_grid[mono_id]
    model_image = jnp.sum(basis_block.astype(jnp.float32) * weights, axis=0) + background
    return science_block - model_image


def body(tile_store, tile_source, tile_slot, shift_cols, spatial_order, science):
    ccd_count = lax.axis_size("ccd")
    strip_count = lax.axis_size("strip")
    device_count = ccd_count * strip_count
    device_id = lax.axis_index("ccd") * strip_count + lax.axis_index("strip")
    tile_count = tile_source.shape[1]
    capacity = -(-tile_count // device_count)
    row_count, col_count = science.shape
    tile_height, tile_width = (tile_store.shape[1], tile_store.shape[2])
    positions = jnp.arange(tile_count)
    same_owner = tile_source[:, :, None] == tile_source[:, None, :]
    earlier = positions[None, :] < positions[:, None]
    rank_table = jnp.sum(same_owner & earlier[None], axis=2)
    held_here = tile_source == device_id
    chosen = held_here[:, None, :] & (rank_table[:, None, :] == jnp.arange(capacity)[None, :, None])
    slot_pick = jnp.sum(jnp.where(chosen, tile_slot[:, None, :], 0), axis=2).reshape(-1)
    filled = jnp.any(chosen, axis=2).reshape(-1).astype(jnp.float32)
    outgoing = jnp.take(tile_store, slot_pick, axis=0) * filled[:, None, None]
    arrived = lax.all_to_all(outgoing, ("ccd", "strip"), split_axis=0, concat_axis=0, tiled=True)
    own_owner = lax.dynamic_index_in_dim(tile_source, device_id, 0, keepdims=False)
    own_rank = lax.dynamic_index_in_dim(rank_table, device_id, 0, keepdims=False)
    received = jnp.take(arrived, own_owner * capacity + own_rank, axis=0)
    template = received.reshape(row_count // tile_height, TW // tile_width, tile_height, tile_width)
    template = template.transpose(0, 2, 1, 3).reshape(row_count, TW)
    padded = with_halo(template, (("strip", 0),), H)
    window = lax.dynamic_slice_in_dim(padded, CM + shift_cols[0] - H, col_count + 2 * H, 1)
    tap_rows = tap_table(H)
    groups = horizontal_pass(window, tap_rows, col_count)
    band_rows = band_tables(tap_rows, H, RB)
    total_rows = row_count * strip_count
    first_row = lax.axis_index("strip") * row_count
    block_count = row_count // RB
    param_count = NB * NSP + NSP

    def gram_block(block_id, carry_pair):
        start_row = block_id * RB
        basis_block = block_basis(groups, band_rows, start_row, RB, H)
        mono_grid = monomials(first_row + start_row, RB, total_rows, col_count)
        design = design_rows(basis_block, mono_grid)
        target = (
            lax.dynamic_slice_in_dim(science, start_row, RB, 0).astype(jnp.bfloat16).reshape(-1)
        )
        gram_part = lax.dot_general(
            design, design, (((1,), (1,)), ((), ())), preferred_element_type=jnp.float32
        )
        rhs_part = jnp.dot(design, target, preferred_element_type=jnp.float32)
        return (carry_pair[0] + gram_part, carry_pair[1] + rhs_part)

    start_pair = (
        jnp.zeros((param_count, param_count), jnp.float32),
        jnp.zeros((param_count,), jnp.float32),
    )
    gram_local, rhs_local = lax.fori_loop(0, block_count, gram_block, start_pair)
    gram_total, rhs_total = lax.psum((gram_local, rhs_local), "strip")
    coeffs = solve_kernel(gram_total, rhs_total, spatial_order[0], NB)

    def diff_block(block_id):
        start_row = block_id * RB
        basis_block = block_basis(groups, band_rows, start_row, RB, H)
        mono_grid = monomials(first_row + start_row, RB, total_rows, col_count)
        science_block = lax.dynamic_slice_in_dim(science, start_row, RB, 0)
        return block_difference(basis_block, mono_grid, coeffs, science_block, NB)

    return lax.map(diff_block, jnp.arange(block_count)).reshape(row_count, col_count)


def solution(mesh):
    placed = (
        P(("ccd", "strip"), None, None),
        P(),
        P(),
        P("ccd"),
        P("ccd"),
        P(("ccd", "strip"), None),
    )
    return jax.shard_map(
        body, mesh=mesh, in_specs=placed, out_specs=P(("ccd", "strip"), None), check_vma=False
    )
```

profile of v0, /device:TPU:0, one launch (start us, length us, event | category | flops | bytes accessed | tf_op | source)
XLA Modules:
  0.0 2248.4 jit_solution(16408839293291734808)
XLA Ops:
  10.4 7.3 all-to-all-start
  36.5 3.7 collective-permute-start
  43.6 4.2 collective-permute-done.1
  48.0 82.4 %while.231 = (s32[]{:T(128)}, f32[38,2048]{1,0:T(8,128)}, f32[23]{0:T(128)}, f32[38,2070]{1,0:T(8,128)S(1)}, s32[]{:T(128)}, /*index=5*/s32[]{:T(128)}) while((s32[]{:T(128)}, f32[38,2048]{1,0:T(8,128)}, f32[23]{0:T(128)}, f32[38,2070]{1,0:T(8,128)S(1)}, s32[]{:T(128)}, /*index=5*/s32[]{:T(128)}) %tuple.518), condition=%wide.region_27.28_spmd.clone, body=%wide.region_26.27_spmd.clone.sunk | while | flops 233475 | bytes 933987 | solution.py:79
  132.0 84.2 %while.230 = (s32[]{:T(128)}, f32[38,2048]{1,0:T(8,128)}, f32[23]{0:T(128)}, f32[38,2070]{1,0:T(8,128)S(1)}, s32[]{:T(128)}, /*index=5*/s32[]{:T(128)}) while((s32[]{:T(128)}, f32[38,2048]{1,0:T(8,128)}, f32[23]{0:T(128)}, f32[38,2070]{1,0:T(8,128)S(1)}, s32[]{:T(128)}, /*index=5*/s32[]{:T(128)}) %tuple.541), condition=%wide.region_25.26_spmd.clone, body=%wide.region_24.25_spmd.clone.sunk | while | flops 233475 | bytes 933987 | solution.py:79
  217.9 49.6 %while.229 = (s32[]{:T(128)}, f32[38,2048]{1,0:T(8,128)S(1)}, f32[23]{0:T(128)}, f32[38,2070]{1,0:T(8,128)S(1)}, s32[]{:T(128)}, /*index=5*/s32[]{:T(128)}) while((s32[]{:T(128)}, f32[38,2048]{1,0:T(8,128)S(1)}, f32[23]{0:T(128)}, f32[38,2070]{1,0:T(8,128)S(1)}, s32[]{:T(128)}, /*index=5*/s32[]{:T(128)}) %tuple.542), condition=%wide.region_23.24_spmd.clone, body=%wide.region_22.23_spmd.clone.sunk | while | flops 233475 | bytes 933987 | solution.py:79
  268.1 47.4 %while.228 = (s32[]{:T(128)}, f32[38,2048]{1,0:T(8,128)S(1)}, f32[23]{0:T(128)}, f32[38,2070]{1,0:T(8,128)S(1)}, s32[]{:T(128)}, /*index=5*/s32[]{:T(128)}) while((s32[]{:T(128)}, f32[38,2048]{1,0:T(8,128)S(1)}, f32[23]{0:T(128)}, f32[38,2070]{1,0:T(8,128)S(1)}, s32[]{:T(128)}, /*index=5*/s32[]{:T(128)}) %tuple.543), condition=%wide.region_20.21_spmd.clone, body=%wide.region_19.20_spmd.clone.sunk | while | flops 233475 | bytes 933987 | solution.py:79
  315.5 33.9 %while.227 = (s32[]{:T(128)}, f32[38,2048]{1,0:T(8,128)S(1)}, f32[23]{0:T(128)S(1)}, f32[38,2070]{1,0:T(8,128)S(1)}, s32[]{:T(128)}, /*index=5*/s32[]{:T(128)}) while((s32[]{:T(128)}, f32[38,2048]{1,0:T(8,128)S(1)}, f32[23]{0:T(128)S(1)}, f32[38,2070]{1,0:T(8,128)S(1)}, s32[]{:T(128)}, /*index=5*/s32[]{:T(128)}) %tuple.555), condition=%wide.region_18.19_spmd.clone, body=%wide.region_17.18_spmd.clone.sunk | while | flops 233475 | bytes 933987 | solution.py:79
  349.5 34.5 %while.226 = (s32[]{:T(128)}, f32[38,2048]{1,0:T(8,128)S(1)}, f32[23]{0:T(128)S(1)}, f32[38,2070]{1,0:T(8,128)S(1)}, s32[]{:T(128)}, /*index=5*/s32[]{:T(128)}) while((s32[]{:T(128)}, f32[38,2048]{1,0:T(8,128)S(1)}, f32[23]{0:T(128)S(1)}, f32[38,2070]{1,0:T(8,128)S(1)}, s32[]{:T(128)}, /*index=5*/s32[]{:T(128)}) %tuple.556), condition=%wide.region_16.17_spmd.clone, body=%wide.region_15.16_spmd.clone.sunk | while | flops 233475 | bytes 933987 | solution.py:79
  384.0 36.9 %while.221 = (s32[]{:T(128)}, f32[38,2048]{1,0:T(8,128)S(1)}, f32[23]{0:T(128)S(1)}, f32[38,2070]{1,0:T(8,128)S(1)}, s32[]{:T(128)}, /*index=5*/s32[]{:T(128)}) while((s32[]{:T(128)}, f32[38,2048]{1,0:T(8,128)S(1)}, f32[23]{0:T(128)S(1)}, f32[38,2070]{1,0:T(8,128)S(1)}, s32[]{:T(128)}, /*index=5*/s32[]{:T(128)}) %tuple.557), condition=%wide.region_5.6_spmd.clone, body=%wide.region_4.5_spmd.clone.sunk | while | flops 233475 | bytes 933987 | solution.py:79
  421.6 34.8 %while.222 = (s32[]{:T(128)}, f32[38,2048]{1,0:T(8,128)S(1)}, f32[23]{0:T(128)S(1)}, f32[38,2070]{1,0:T(8,128)S(1)}, s32[]{:T(128)}, /*index=5*/s32[]{:T(128)}) while((s32[]{:T(128)}, f32[38,2048]{1,0:T(8,128)S(1)}, f32[23]{0:T(128)S(1)}, f32[38,2070]{1,0:T(8,128)S(1)}, s32[]{:T(128)}, /*index=5*/s32[]{:T(128)}) %tuple.547), condition=%wide.region_7.8_spmd.clone, body=%wide.region_6.7_spmd.clone.sunk | while | flops 233475 | bytes 933987 | solution.py:79
  456.3 36.2 %while.223 = (s32[]{:T(128)}, f32[38,2048]{1,0:T(8,128)S(1)}, f32[23]{0:T(128)S(1)}, f32[38,2070]{1,0:T(8,128)S(1)}, s32[]{:T(128)}, /*index=5*/s32[]{:T(128)}) while((s32[]{:T(128)}, f32[38,2048]{1,0:T(8,128)S(1)}, f32[23]{0:T(128)S(1)}, f32[38,2070]{1,0:T(8,128)S(1)}, s32[]{:T(128)}, /*index=5*/s32[]{:T(128)}) %tuple.548), condition=%wide.region_9.10_spmd.clone, body=%wide.region_8.9_spmd.clone.sunk | while | flops 233475 | bytes 933987 | solution.py:79
  492.5 31.1 %while.224 = (s32[]{:T(128)}, f32[38,2048]{1,0:T(8,128)S(1)}, f32[23]{0:T(128)S(1)}, f32[38,2070]{1,0:T(8,128)S(1)}, s32[]{:T(128)}, /*index=5*/s32[]{:T(128)}) while((s32[]{:T(128)}, f32[38,2048]{1,0:T(8,128)S(1)}, f32[23]{0:T(128)S(1)}, f32[38,2070]{1,0:T(8,128)S(1)}, s32[]{:T(128)}, /*index=5*/s32[]{:T(128)}) %tuple.549), condition=%wide.region_11.12_spmd.clone, body=%wide.region_10.11_spmd.clone.sunk | while | flops 233475 | bytes 933987 | solution.py:79
  523.7 34.4 %while.225 = (s32[]{:T(128)}, f32[38,2048]{1,0:T(8,128)S(1)}, f32[23]{0:T(128)S(1)}, f32[38,2070]{1,0:T(8,128)S(1)}, s32[]{:T(128)}, /*index=5*/s32[]{:T(128)}) while((s32[]{:T(128)}, f32[38,2048]{1,0:T(8,128)S(1)}, f32[23]{0:T(128)S(1)}, f32[38,2070]{1,0:T(8,128)S(1)}, s32[]{:T(128)}, /*index=5*/s32[]{:T(128)}) %tuple.550), condition=%wide.region_13.14_spmd.clone, body=%wide.region_12.13_spmd.clone.sunk | while | flops 233475 | bytes 933987 | solution.py:79
  562.5 102.6 %while.232 = (s32[]{:T(128)}, f32[168,168]{1,0:T(8,128)}, f32[168]{0:T(256)S(1)}, bf16[5,38,2048]{2,1,0:T(8,128)(2,1)}, bf16[5,4,26]{2,0,1:T(8,128)(2,1)S(1)}, /...) while((s32[]{:T(128)}, f32[168,168]{1,0:T(8,128)}, ...), condition=%wide.region_29.30_spmd.clone, body=%wide.region_28.29_spmd.clone.sunk | while | flops 486618624 | bytes 44266800 | solution.py:238
  574.3 9.2 concatenate.104
  583.5 3.7 convolution_add_fusion.2
  600.1 9.2 concatenate.104
  609.2 3.7 convolution_add_fusion.2
  625.7 9.2 concatenate.104
  634.8 3.7 convolution_add_fusion.2
  651.3 9.2 concatenate.104
  660.4 3.7 convolution_add_fusion.2
  666.8 20.5 psum.14
  687.3 49.9 %all-reduce.4.cloned.1.call-done = f32[168,168]{0,1:T(8,128)} async-done(((f32[168,168]{0,1:T(8,128)}), f32[168,168]{0,1:T(8,128)}) %all-reduce.4.cloned.1.call-update) | async-done | bytes 112912 | tf_op jit(solution)/shard_map/psum | solution.py:239
  738.2 2.8 gather_fusion.2
  743.2 11.7 cholesky.50
  754.9 9.8 custom-call.11
  765.1 3.6 cholesky.108
  772.1 706.6 %while.218 = (s32[]{:T(128)}, f32[168]{0:T(256)S(1)}, f32[168]{0:T(256)S(1)}, f32[168,168]{1,0:T(8,128)S(1)}, s32[]{:T(128)}, /*index=5*/s32[]{:T(128)}, s32[]{:T(128)}) while((s32[]{:T(128)}, f32[168]{0:T(256)S(1)}, f32[168]{0:T(256)S(1)}, f32[168,168]{1,0:T(8,128)S(1)}, s32[]{:T(128)}, /*index=5*/s32[]{:T(128)}, s32[]{:T(128)}) %tuple.530), condition=%wide.region_38.39_spmd, body=%wide.region_36.38_spmd.sunk | while | flops 340 | bytes 2849 | solution.py:142
  1478.7 706.6 %while.219 = (s32[]{:T(128)}, f32[168]{0:T(256)S(1)}, f32[168]{0:T(256)S(1)}, f32[168,168]{0,1:T(8,128)S(1)}, s32[]{:T(128)}, /*index=5*/s32[]{:T(128)}, s32[]{:T(128)}, s32[]{:T(128)}) while((s32[]{:T(128)}, f32[168]{0:T(256)S(1)}, f32[168]{0:T(256)S(1)}, f32[168,168]{0,1:T(8,128)S(1)}, s32[]{:T(128)}, /*index=5*/s32[]{:T(128)}, ...), condition=%wide.region_41.42_spmd, body=%wide.region_39.41_spmd.sunk | while | flops 344 | bytes 2903 | solution.py:157
  2185.3 55.6 %while.220 = (s32[]{:T(128)}, f32[4,4,2048]{2,1,0:T(4,128)S(1)}, s32[4]{0:T(128)S(1)}, f32[16,2048]{1,0:T(8,128)}, bf16[5,38,2048]{2,1,0:T(8,128)(2,1)}, /*index...) while((s32[]{:T(128)}, f32[4,4,2048]{2,1,0:T(4,128)S(1)}, ...), condition=%wide.region_44.45_spmd, body=%wide.region_42.44_spmd.sunk | while | flops 21637180 | bytes 5037416 | solution.py:249
  (2677 shorter events, 1352.3 us)
Async XLA Ops:
  6.5 2.4 copy-start
  10.4 23.7 %all-to-all-start = ((f32[32,16,128]{2,1,0:T(8,128)}), f32[32,16,128]{2,1,0:T(8,128)S(1)}, u32[]{:S(2)}, u32[]{:S(2)}) async-start(f32[32,16,128]{2,1,0:T(8,128)} %select_multiply_fusion), calls=%async_computation | async-start | bytes 524288 | tf_op jit(solution)/shard_map/all_to_all | solution.py:204
  17.7 719.5 %all-reduce.4.cloned.1.call-start = ((), (), s32[]{:S(2)}) async-start(), calls=%async_computation.1 | async-start | bytes 344064 | tf_op jit(solution)/shard_map/psum | solution.py:239
  36.5 7.1 collective-permute-start
  40.3 7.5 collective-permute-start.1
  268.1 47.4 %copy-start.8 = (f32[23]{0:T(128)S(1)}, f32[23]{0:T(128)}, u32[]{:S(2)}) copy-start(f32[23]{0:T(128)} %get-tuple-element.2801) | copy-start | bytes 280
  315.5 34.0 %copy-start.9 = (f32[23]{0:T(128)S(1)}, f32[23]{0:T(128)}, u32[]{:S(2)}) copy-start(f32[23]{0:T(128)} %broadcast_divide_fusion.3) | copy-start | bytes 280
  349.5 34.5 %copy-start.10 = (f32[23]{0:T(128)S(1)}, f32[23]{0:T(128)}, u32[]{:S(2)}) copy-start(f32[23]{0:T(128)} %broadcast_divide_fusion.5) | copy-start | bytes 280
  523.6 37.2 %copy-start.2 = (bf16[1,38,2048]{2,1,0:T(8,128)(2,1)S(1)}, bf16[1,38,2048]{2,1,0:T(8,128)(2,1)}, u32[]{:S(2)}) copy-start(bf16[1,38,2048]{2,1,0:T(8,128)(2,1)} %convert_bitcast_fusion) | copy-start | bytes 466948
  523.6 37.2 %copy-start.3 = (bf16[1,38,2048]{2,1,0:T(8,128)(2,1)S(1)}, bf16[1,38,2048]{2,1,0:T(8,128)(2,1)}, u32[]{:S(2)}) copy-start(bf16[1,38,2048]{2,1,0:T(8,128)(2,1)} %convert_bitcast_fusion.1) | copy-start | bytes 466948
  523.6 37.2 %copy-start.4 = (bf16[1,38,2048]{2,1,0:T(8,128)(2,1)S(1)}, bf16[1,38,2048]{2,1,0:T(8,128)(2,1)}, u32[]{:S(2)}) copy-start(bf16[1,38,2048]{2,1,0:T(8,128)(2,1)} %convert_bitcast_fusion.2) | copy-start | bytes 466948
  574.3 9.2 copy-start.5
  583.5 3.8 copy-start.1
  587.2 1.0 copy-start.6
  600.1 9.2 copy-start.5
  609.2 3.8 copy-start.1
  612.9 1.0 copy-start.6
  625.7 9.2 copy-start.5
  634.8 3.8 copy-start.1
  638.5 1.0 copy-start.6
  651.3 9.2 copy-start.5
  660.4 3.8 copy-start.1
  664.1 1.0 copy-start.6
  666.8 1518.4 %copy-start.7 = (f32[4,4,2048]{2,1,0:T(4,128)S(1)}, f32[4,4,2048]{2,1,0:T(4,128)}, u32[]{:S(2)}) copy-start(f32[4,4,2048]{2,1,0:T(4,128)} %custom-call.33) | copy-start | bytes 393220
Sparse Core Ops, SparseCore 0:
  667.0 70.2 all-reduce.3
where the time goes:
time: 2270 us; the launch traced here: 2250 us
  local copies, waits for them, and re-layouts  772 us (34%)
  loops' own time  715 us (31%)
  other arithmetic  606 us (27%)
  waiting for transfers between devices  55 us (2%)
  matrix products  50.7 us (2%)
    another operation x1, loops' own time, forward_solve(): return lax.fori_loop(0, count, step_down, jnp.zeros((count,), jnp.float32))  352 us
    another operation x1, loops' own time, backward_solve(): return lax.fori_loop(0, count, step_up, jnp.zeros((count,), jnp.float32))  352 us
    add x253, other arithmetic, add_tap(): running + taps_now[tap_id] * lax.dynamic_slice_in_dim(window, tap_id, out...  286 us
    dynamic_slice x253, local copies, waits for them, and re-layouts, add_tap(): taps_now[tap_id] * lax.dynamic_slice_in_dim(window, tap_id, out_cols, 1)  214 us
    reduce_sum x168, other arithmetic, step_up(): partial_value = jnp.sum(column_now * known)  115 us
    reduce_sum x168, other arithmetic, step_down(): partial_value = jnp.sum(row_now * known)  115 us
    dynamic_slice x168, local copies, waits for them, and re-layouts, step_down(): row_now[row_id]  110 us
    dynamic_slice x168, local copies, waits for them, and re-layouts, step_up(): column_now[row_id]  110 us
  transfers between devices with their start and end apart: 4, of which 3 were waited for; matrix products, arithmetic and copies ran while one was open for 1% of the time, Pallas kernels for 0%

commit v1 on v0

v1 whole, which is shorter than its diff:
```python
import math

import jax
import jax.numpy as jnp
from jax import lax
from jax.experimental import pallas as pl
from jax.experimental.pallas import tpu as pltpu
from jax.sharding import PartitionSpec as P

H = 11
CM = 128
TW = 2304
LANES = 128
SLOTS = 32

gauss_sigmas = (0.7, 1.5, 3.0)
poly_degrees = (4, 2, 2)
mono_degrees = (0, 1, 1, 2, 2, 2)
mono_powers = ((0, 0), (1, 0), (0, 1), (2, 0), (1, 1), (0, 2))
ridge_weight = 0.05

filters = [(g, n) for g, top in enumerate(poly_degrees) for n in range(top + 1)]
basis_list = [
    (g, i, j) for g, top in enumerate(poly_degrees) for i in range(top + 1) for j in range(top + 1 - i)
]
NB = len(basis_list)
NF = len(filters)
ONE = NB
SCI = NB + 1
moment_keys = [(a, c) for c in range(5) for a in range(5 - c)]
NQ = len(mono_powers)
PIV = 4
VMEM_BYTES = 56 * 1024 * 1024


def envelope_norm(sigma):
    return sum(math.exp(-a * a / (2.0 * sigma * sigma)) for a in range(-H, H + 1))


def iota(shape, dim):
    return lax.broadcasted_iota(jnp.int32, shape, dim)


def split_two(value):
    high = value.astype(jnp.bfloat16)
    low = (value - high.astype(jnp.float32)).astype(jnp.bfloat16)
    return high, low


def pack_kernel(store_ref, source_ref, slot_ref, out_ref):
    me = lax.axis_index("ccd") * lax.axis_size("strip") + lax.axis_index("strip")
    strips, tiles = source_ref.shape
    rows = store_ref.shape[1]

    def one_strip(strip, carry):
        slot = jnp.int32(0)
        for t in range(tiles):
            slot = slot + jnp.where(source_ref[strip, t] == me, slot_ref[strip, t], 0)
        after = lax.rem(strip + 1, strips)
        before = lax.rem(strip + strips - 1, strips)
        out_ref[strip, H : H + rows, :] = store_ref[slot]
        out_ref[after, 0:H, :] = store_ref[slot, rows - H : rows, :]
        out_ref[before, H + rows : 2 * H + rows, :] = store_ref[slot, 0:H, :]
        return carry

    lax.fori_loop(0, strips, one_strip, 0)


def table_kernel(horizontal_high_ref, horizontal_low_ref, vertical_ref, *, rows, high):
    offset = (iota((2 * LANES, LANES), 0) - iota((2 * LANES, LANES), 1) - H).astype(jnp.float32)
    inside = jnp.abs(offset) <= H
    for f, (g, n) in enumerate(filters):
        sigma = gauss_sigmas[g]
        tap = jnp.exp(-offset * offset / (2.0 * sigma * sigma)) * (1.0 / envelope_norm(sigma))
        for _ in range(n):
            tap = tap * (offset * (1.0 / sigma))
        tap = jnp.where(inside, tap, 0.0)
        tap_high, tap_low = split_two(tap)
        horizontal_high_ref[:, f * LANES : (f + 1) * LANES] = tap_high
        horizontal_low_ref[:, f * LANES : (f + 1) * LANES] = tap_low
    width = vertical_ref.shape[1]
    slot = iota((SLOTS, width), 0)
    column = iota((SLOTS, width), 1)
    wanted = jnp.full((SLOTS, width), -1, jnp.int32)
    degree = jnp.zeros((SLOTS, width), jnp.int32)
    scale = jnp.ones((SLOTS, width), jnp.float32)
    weight = jnp.zeros((SLOTS, width), jnp.float32)
    for b, (g, i, j) in enumerate(basis_list):
        here = slot == b
        wanted = jnp.where(here, filters.index((g, i)), wanted)
        degree = jnp.where(here, j, degree)
        scale = jnp.where(here, 1.0 / gauss_sigmas[g], scale)
        weight = jnp.where(here, 1.0 / envelope_norm(gauss_sigmas[g]), weight)
    row_in = column - wanted * high
    matched = (row_in >= 0) & (row_in < high)
    for r in range(rows):
        a = row_in - (r + H)
        z = a.astype(jnp.float32) * scale
        tap = jnp.exp(-0.5 * z * z) * weight
        square = z * z
        power = jnp.where(degree == 1, z, jnp.where(degree == 2, square, 1.0))
        power = jnp.where(degree == 3, square * z, jnp.where(degree == 4, square * square, power))
        keep = matched & (jnp.abs(a) <= H)
        vertical_ref[r * SLOTS : (r + 1) * SLOTS, :] = jnp.where(keep, tap * power, 0.0).astype(jnp.bfloat16)


def u_row(cols):
    return 2.0 * (iota((1, cols), 1).astype(jnp.float32) + 0.5) / cols - 1.0


def basis_kernel(
    arrived_ref, source_ref, shift_ref, science_ref, high_ref, low_ref, vertical_ref,
    basis_out_ref, moment_ref, filtered_ref, basis_ref, sem,
):
    strip_count = lax.axis_size("strip")
    strip = lax.axis_index("strip")
    me = lax.axis_index("ccd") * strip_count + strip
    rows, cols = science_ref.shape
    high = arrived_ref.shape[1]
    strips, tiles = source_ref.shape
    blocks = cols // LANES
    above = jnp.maximum(me - 1, 0)
    below = jnp.minimum(me + 1, strips - 1)
    row_id = iota((high, LANES), 0)
    lane_id = iota((high, LANES), 1)
    is_above = row_id < H
    is_own = row_id < H + rows
    first_row = jnp.where(strip == 0, H, 0)
    last_row = jnp.where(strip == strip_count - 1, H + rows, 2 * H + rows)
    present = (row_id >= first_row) & (row_id < last_row)
    start = CM - H + shift_ref[0]
    skip = jnp.where(start >= LANES, 1, 0)
    offset = start - skip * LANES
    turn = lax.rem(LANES - offset, LANES)
    stays = lane_id < LANES - offset
    turned = []
    for w in range(blocks + 2):
        t = jnp.minimum(w + skip, tiles - 1)
        tile = jnp.where(
            is_above,
            arrived_ref[source_ref[above, t]],
            jnp.where(is_own, arrived_ref[source_ref[me, t]], arrived_ref[source_ref[below, t]]),
        )
        turned.append(pltpu.roll(jnp.where(present, tile, 0.0), turn, 1))
    window = [split_two(jnp.where(stays, turned[w], turned[w + 1])) for w in range(blocks + 1)]
    left = []
    for w in range(blocks):
        (h0, l0), (h1, l1) = window[w], window[w + 1]
        left.append(jnp.concatenate([h0, h1, l0, l1, h0, h1], axis=1))
    left = jnp.concatenate(left, axis=0)
    right = jnp.concatenate([high_ref[...], high_ref[...], low_ref[...]], axis=0)
    filtered_ref[...] = jnp.dot(left, right, preferred_element_type=jnp.float32)

    slot_id = iota((rows * SLOTS, 2 * LANES), 0) & (SLOTS - 1)
    copies = []
    for pair in range(blocks // 2):
        halves = []
        for w in (2 * pair, 2 * pair + 1):
            halves.append(
                jnp.concatenate(
                    [filtered_ref[w * high : (w + 1) * high, f * LANES : (f + 1) * LANES] for f in range(NF)],
                    axis=0,
                ).astype(jnp.bfloat16)
            )
        block = jnp.dot(
            vertical_ref[...], jnp.concatenate(halves, axis=1), preferred_element_type=jnp.float32
        )
        at = slice(pair * 2 * LANES, (pair + 1) * 2 * LANES)
        science = jnp.broadcast_to(science_ref[:, at][:, None, :], (rows, SLOTS, 2 * LANES))
        science = science.reshape(rows * SLOTS, 2 * LANES)
        block = jnp.where(slot_id == ONE, 1.0, jnp.where(slot_id == SCI, science, block))
        basis_ref[:, at] = block.astype(jnp.bfloat16)
    copy = pltpu.make_async_copy(basis_ref, basis_out_ref, sem)
    copy.start()

    u = u_row(cols)
    square = u * u
    totals = [None] * 5
    for r in range(rows):
        here = basis_ref[r * SLOTS : (r + 1) * SLOTS, :]
        wide = here.astype(jnp.float32)
        design = jnp.concatenate(
            [here, (wide * u).astype(jnp.bfloat16), (wide * square).astype(jnp.bfloat16)], axis=0
        )
        product = lax.dot_general(
            design, design, (((1,), (1,)), ((), ())), preferred_element_type=jnp.float32
        )
        v = 2.0 * ((strip * rows + r).astype(jnp.float32) + 0.5) / (rows * strip_count) - 1.0
        for c in range(5):
            totals[c] = product if totals[c] is None else totals[c] + product
            product = product * v
    placed = []
    for a, c in moment_keys:
        first, second = (a, 0) if a < 3 else (a - 2, 2)
        placed.append(
            totals[c][first * SLOTS : (first + 1) * SLOTS, second * SLOTS : (second + 1) * SLOTS]
        )
    placed.append(jnp.zeros((SLOTS, SLOTS), jnp.float32))
    for p in range(4):
        chunk = jnp.concatenate(placed[4 * p : 4 * p + 4], axis=1)
        for k in range(moment_ref.shape[0]):
            moment_ref[k, p * SLOTS : (p + 1) * SLOTS, :] = chunk
    copy.wait()


def solve_kernel(moment_ref, order_ref, science_ref, basis_any_ref, out_ref, system_ref, basis_ref, sem):
    strip_count = lax.axis_size("strip")
    strip = lax.axis_index("strip")
    rows, cols = science_ref.shape
    copy = pltpu.make_async_copy(basis_any_ref, basis_ref, sem)
    copy.start()
    order = order_ref[0]
    total = moment_ref[0]
    for k in range(1, moment_ref.shape[0]):
        total = total + moment_ref[k]
    lane = iota((SLOTS, LANES), 1)
    lane_slot = lane & (SLOTS - 1)
    lane_group = lane // SLOTS
    row_slot = iota((SLOTS, LANES), 0)

    def active(slot, q):
        return ((slot < NB) & (mono_degrees[q] <= order)) | (slot == ONE)

    def moved(key, to_lane, from_lane):
        at = moment_keys.index(key)
        piece = total[(at // 4) * SLOTS : (at // 4 + 1) * SLOTS, :]
        by = (to_lane - from_lane - (at % 4) * SLOTS) % LANES
        return pltpu.roll(piece, by, 1) if by else piece

    for q, (aq, cq) in enumerate(mono_powers):
        tiles = [jnp.zeros((SLOTS, LANES), jnp.float32) for _ in range(2)]
        for k, (ak, ck) in enumerate(mono_powers):
            keep = (lane_group == k % 4) & active(lane_slot, k)
            tiles[k // 4] = jnp.where(keep, moved((aq + ak, cq + ck), (k % 4) * SLOTS, 0), tiles[k // 4])
        tiles[1] = jnp.where(lane == 2 * SLOTS, moved((aq, cq), 2 * SLOTS, SCI), tiles[1])
        row_on = active(row_slot, q)
        for side in range(2):
            tile = jnp.where(row_on, tiles[side], 0.0)
            if q // 4 == side:
                diagonal = lane == row_slot + (q % 4) * SLOTS
                weight = jnp.where(row_on, tile, 1.0) * (1.0 + ridge_weight)
                tile = jnp.where(diagonal, weight, tile)
            system_ref[q * SLOTS : (q + 1) * SLOTS, side * LANES : (side + 1) * LANES] = tile

    def eliminate(q, carry):
        base = pl.multiple_of(q * SLOTS, SLOTS)
        for p in range(0, NB + 1, PIV):
            whole = system_ref[...]
            around = system_ref[pl.ds(base + (p // 8) * 8, 8), :]
            pivot_rows = [around[p % 8 + i : p % 8 + i + 1, :] for i in range(PIV)]
            left = [
                [jnp.broadcast_to(pivot_rows[i][:, p + j : p + j + 1], (1, LANES)) for j in range(PIV)]
                for i in range(PIV)
            ]
            ready = [list(jnp.split(row, 2, axis=1)) for row in pivot_rows]
            for i in range(PIV):
                inverse = 1.0 / left[i][i]
                left[i] = [x * inverse for x in left[i]]
                ready[i] = [x * inverse for x in ready[i]]
                for k in range(PIV):
                    if k != i:
                        factor = left[k][i]
                        left[k] = [x - factor * y for x, y in zip(left[k], left[i])]
                        ready[k] = [x - factor * y for x, y in zip(ready[k], ready[i])]
            ready = [jnp.concatenate(row, axis=1) for row in ready]
            for j in range(PIV):
                whole = whole - whole_column(system_ref, p + j) * ready[j]
            system_ref[...] = whole
            for i in range(PIV):
                system_ref[pl.ds(base + p + i, 1), :] = ready[i]
        system_ref[...] = pltpu.roll(system_ref[...], 2 * LANES - SLOTS, 1)
        return carry

    def whole_column(ref, at):
        return jnp.broadcast_to(ref[:, at : at + 1], ref.shape)

    lax.fori_loop(0, NQ, eliminate, 0)
    solved = system_ref[:, 0:1]
    turned = []
    for q in range(NQ):
        part = solved[q * SLOTS : (q + 1) * SLOTS]
        part = jnp.broadcast_to(jnp.concatenate([part] * (LANES // SLOTS), axis=0), (LANES, LANES))
        turned.append(jnp.transpose(part)[0:rows, :])
    row = iota((rows, LANES), 0)
    v = 2.0 * ((strip * rows + row).astype(jnp.float32) + 0.5) / (rows * strip_count) - 1.0
    group = iota((rows, LANES), 1) // SLOTS
    weights = [jnp.zeros((rows, LANES), jnp.float32) for _ in range(3)]
    for q, (a, c) in enumerate(mono_powers):
        weights[a] = weights[a] + turned[q] * (v * v if c == 2 else v if c else jnp.ones_like(v))
    spread = jnp.concatenate(
        [
            jnp.concatenate(
                [jnp.where(group + m * (LANES // SLOTS) == row, w, 0.0) for m in range(rows * SLOTS // LANES)],
                axis=1,
            )
            for w in weights
        ],
        axis=0,
    )
    spread_high, spread_low = split_two(spread)
    spread = jnp.concatenate([spread_high, spread_low], axis=0)
    copy.wait()
    sums = jnp.dot(spread, basis_ref[...], preferred_element_type=jnp.float32)
    u = u_row(cols)
    model = [sums[a * rows : (a + 1) * rows] + sums[(a + 3) * rows : (a + 4) * rows] for a in range(3)]
    out_ref[...] = science_ref[...] - (model[0] + u * (model[1] + u * model[2]))


def body(tile_store, tile_source, tile_slot, shift_cols, spatial_order, science):
    strip_count = lax.axis_size("strip")
    device_count = lax.axis_size("ccd") * strip_count
    rows, cols = science.shape
    high = -(-(rows + 2 * H) // 8) * 8
    vmem = pl.BlockSpec(memory_space=pltpu.VMEM)
    smem = pl.BlockSpec(memory_space=pltpu.SMEM)
    hbm = pl.BlockSpec(memory_space=pl.ANY)
    params = pltpu.CompilerParams(vmem_limit_bytes=VMEM_BYTES)

    outgoing = pl.pallas_call(
        pack_kernel,
        out_shape=jax.ShapeDtypeStruct((device_count, high, LANES), jnp.float32),
        in_specs=[vmem, smem, smem],
        out_specs=vmem,
        compiler_params=params,
        name="pack",
    )(tile_store, tile_source, tile_slot)
    arrived = lax.all_to_all(outgoing, ("ccd", "strip"), split_axis=0, concat_axis=0, tiled=True)

    taps_high, taps_low, vertical = pl.pallas_call(
        lambda *refs: table_kernel(*refs, rows=rows, high=high),
        out_shape=(
            jax.ShapeDtypeStruct((2 * LANES, NF * LANES), jnp.bfloat16),
            jax.ShapeDtypeStruct((2 * LANES, NF * LANES), jnp.bfloat16),
            jax.ShapeDtypeStruct((rows * SLOTS, NF * high), jnp.bfloat16),
        ),
        out_specs=(vmem, vmem, vmem),
        compiler_params=params,
        name="tables",
        cost_estimate=pl.CostEstimate(flops=10_000_000, bytes_accessed=2_000_000, transcendentals=1_000_000),
    )()

    basis, moments = pl.pallas_call(
        basis_kernel,
        out_shape=(
            jax.ShapeDtypeStruct((rows * SLOTS, cols), jnp.bfloat16),
            jax.ShapeDtypeStruct((strip_count, 4 * SLOTS, LANES), jnp.float32),
        ),
        in_specs=[vmem, smem, smem, vmem, vmem, vmem, vmem],
        out_specs=(hbm, vmem),
        scratch_shapes=[
            pltpu.VMEM((cols // LANES * high, NF * LANES), jnp.float32),
            pltpu.VMEM((rows * SLOTS, cols), jnp.bfloat16),
            pltpu.SemaphoreType.DMA,
        ],
        compiler_params=params,
        name="basis",
    )(arrived, tile_source, shift_cols, science, taps_high, taps_low, vertical)
    gathered = lax.all_to_all(moments, "strip", split_axis=0, concat_axis=0, tiled=True)

    return pl.pallas_call(
        solve_kernel,
        out_shape=jax.ShapeDtypeStruct((rows, cols), jnp.float32),
        in_specs=[vmem, smem, vmem, hbm],
        out_specs=vmem,
        scratch_shapes=[
            pltpu.VMEM((NQ * SLOTS, 2 * LANES), jnp.float32),
            pltpu.VMEM((rows * SLOTS, cols), jnp.bfloat16),
            pltpu.SemaphoreType.DMA,
        ],
        compiler_params=params,
        name="solve",
    )(gathered, spatial_order, science, basis)


def solution(mesh):
    placed = (
        P(("ccd", "strip"), None, None),
        P(),
        P(),
        P("ccd"),
        P("ccd"),
        P(("ccd", "strip"), None),
    )
    return jax.shard_map(
        body, mesh=mesh, in_specs=placed, out_specs=P(("ccd", "strip"), None), check_vma=False
    )
```

time: 2270 us -> 72.6 us (0.03)
  local copies, waits for them, and re-layouts: 772 us -> 4.4 us
  loops' own time: 715 us -> 0 us
  other arithmetic: 606 us -> 0 us
  matrix products: 50.7 us -> 0 us
  Pallas kernels: 0 us -> 25.7 us
  waiting for transfers between devices: 55 us -> 29.9 us
    another operation x15 -> x0, loops' own time: 715 us -> none  [the longest x1 352 us: forward_solve(): return lax.fori_loop(0, count, step_down, jnp.zeros((count,), jnp.float32))]
    dynamic_slice x1265 -> x0, local copies, waits for them, and re-layouts: 655 us -> none  [the longest x253 214 us: add_tap(): taps_now[tap_id] * lax.dynamic_slice_in_dim(window, tap_id, out_cols, 1)]
    add x264 -> x0, other arithmetic: 297 us -> none  [the longest x253 286 us: add_tap(): running + taps_now[tap_id] * lax.dynamic_slice_in_dim(window, tap_id, out...]
    reduce_sum x345 -> x0, other arithmetic: 238 us -> none  [the longest x168 115 us: step_up(): partial_value = jnp.sum(column_now * known)]
    dot_general x35 -> x0, matrix products: 50.3 us -> none  [the longest x24 31.7 us: block_basis(): jnp.einsum('jrk,ikx->ijrx', band_rows[group_id], rows_in, preferred_eleme...]
    psum x1 -> x0, waiting for transfers between devices: 49.9 us -> none  [body(): gram_total, rhs_total = lax.psum((gram_local, rhs_local), 'strip')]
    concatenate x80 -> x0, local copies, waits for them, and re-layouts: 47.1 us -> none  [the longest x4 36.6 us: design_rows(): return jnp.concatenate([kernel_part, back_part], axis=0)]
    dynamic_update_slice x336 -> x0, local copies, waits for them, and re-layouts: 38.6 us -> none  [the longest x168 19.3 us: step_down(): return lax.dynamic_update_index_in_dim(known, value_now, row_id, 0)]
  transfers between devices with their start and end apart: 4 -> 2, of which waited for: 3 -> 2; matrix products, arithmetic and copies ran while one was open for 1% -> 0% of each run, Pallas kernels for 0% -> 3%
where the time goes in v1:
time: 72.6 us; the launch traced here: 72.1 us
  waiting for transfers between devices  29.9 us (41%)
  Pallas kernels  25.7 us (35%)
  starting transfers between devices  10.8 us (15%)
  local copies, waits for them, and re-layouts  4.4 us (6%)
  between operations  1.32 us (2%)
    all_to_all x1, waiting for transfers between devices, body(): lax.all_to_all(outgoing, ('ccd', 'strip'), split_axis=0, concat_axis=0, t...  16.3 us
    all_to_all x1, waiting for transfers between devices, body(): lax.all_to_all(moments, 'strip', split_axis=0, concat_axis=0, tiled=True)  13.6 us
    pallas_call x1, Pallas kernels, body(): pl.pallas_call(solve_kernel, out_shape=jax.ShapeDtypeStruct((rows, cols),...  12.5 us
    pallas_call x1, Pallas kernels, body(): pl.pallas_call(basis_kernel, out_shape=(jax.ShapeDtypeStruct((rows * SLOT...  7.57 us
    all_to_all x1, starting transfers between devices, body(): lax.all_to_all(outgoing, ('ccd', 'strip'), split_axis=0, concat_axis=0, t...  7.3 us
    unnamed x6, local copies, waits for them, and re-layouts  4.4 us
    all_to_all x1, starting transfers between devices, body(): lax.all_to_all(moments, 'strip', split_axis=0, concat_axis=0, tiled=True)  3.5 us
    pallas_call x1, Pallas kernels, body(): pl.pallas_call(pack_kernel, out_shape=jax.ShapeDtypeStruct((device_count,...  3.42 us
  transfers between devices with their start and end apart: 2, of which 2 were waited for; matrix products, arithmetic and copies ran while one was open for 0% of the time, Pallas kernels for 3%

profile of v1, /device:TPU:0, one launch (start us, length us, event | category | flops | bytes accessed | tf_op | source)
XLA Modules:
  0.0 72.1 jit_solution(15482437914016452023)
XLA Ops:
  0.0 1.4 %copy.7.source_ref = s32[32,18]{1,0:T(8,128)} copy(s32[32,18]{0,1:T(8,128)} %param.7) | data formatting | bytes 4608 | tf_op args[1]
  1.4 1.4 %copy.8.slot_ref = s32[32,18]{1,0:T(8,128)} copy(s32[32,18]{0,1:T(8,128)} %param.8) | data formatting | bytes 4608 | tf_op args[2]
  2.8 3.4 %pack.1 = f32[32,40,128]{2,1,0:T(8,128)} custom-call(f32[18,16,128]{2,1,0:T(8,128)} %store_ref.1, s32[32,18]{1,0:T(8,128)} %copy.7.source_ref, s32[32,18]{1,0:T(8,128)} %copy.8.slot_ref), custom_call_target="tpu_custom_call" | custom-call | tf_op jit(solution)/shard_map/pack/pallas_call | solution.py:319
  6.2 7.3 %all-to-all-start = ((f32[32,40,128]{2,1,0:T(8,128)}), f32[32,40,128]{2,1,0:T(8,128)S(1)}, u32[]{:S(2)}, u32[]{:S(2)}) async-start(f32[32,40,128]{2,1,0:T(8,128)} %pack.1), calls=%async_computation | async-start | bytes 1310720 | tf_op jit(solution)/shard_map/all_to_all | solution.py:327
  14.1 2.2 %tables.1 = (bf16[256,1408]{1,0:T(8,128)(2,1)}, bf16[256,1408]{1,0:T(8,128)(2,1)}, bf16[512,440]{1,0:T(8,128)(2,1)}) custom-call(), custom_call_target="tpu_custom_call" | custom-call | flops 10000000 | bytes 2000000 | tf_op jit(solution)/shard_map/tables/pallas_call | solution.py:329
  16.3 16.3 %all-to-all-done.arrived_ref = f32[32,40,128]{2,1,0:T(8,128)S(1)} async-done(((f32[32,40,128]{2,1,0:T(8,128)}), f32[32,40,128]{2,1,0:T(8,128)S(1)}, u32[]{:S(2)}, u32[]{:S(2)}) %all-to-all-start) | async-done | bytes 655392 | tf_op jit(solution)/shard_map/all_to_all | solution.py:327
  32.7 0.0 copy-start
  32.7 0.8 %copy-done = f32[32,40,128]{2,1,0:T(8,128)} copy-done((f32[32,40,128]{2,1,0:T(8,128)}, f32[32,40,128]{2,1,0:T(8,128)S(1)}, u32[]{:S(2)}) %copy-start) | copy-done | bytes 655384
  33.5 7.6 %basis.1 = (bf16[512,2048]{1,0:T(8,128)(2,1)}, f32[8,128,128]{2,1,0:T(8,128)}) custom-call(f32[32,40,128]{2,1,0:T(8,128)} %copy-done, s32[32,18]{1,0:T(8,128)} %copy.7.source_ref, s32[1]{0:T(128)S(6)} %copy.10.shift_ref, f32[16,2048]{1,0:T(8,128)} %science_ref.3, bf16[256,1408]{1,0:T(8,128)(2,1)} %get-tuple-element.10.high_ref, ...), custom_call_target="tpu_custom_call" | custom-call | tf_op jit(solution)/shard_map/basis/pallas_call | solution.py:342
  41.1 3.5 %all-to-all-start.1 = ((f32[8,128,128]{2,1,0:T(8,128)}), f32[8,128,128]{2,1,0:T(8,128)S(1)}, u32[]{:S(2)}, u32[]{:S(2)}) async-start(f32[8,128,128]{2,1,0:T(8,128)} %get-tuple-element.13), calls=%async_computation.1 | async-start | bytes 1048576 | tf_op jit(solution)/shard_map/all_to_all | solution.py:358
  45.2 13.6 %all-to-all-done.1.moment_ref = f32[8,128,128]{2,1,0:T(8,128)S(1)} async-done(((f32[8,128,128]{2,1,0:T(8,128)}), f32[8,128,128]{2,1,0:T(8,128)S(1)}, u32[]{:S(2)}, u32[]{:S(2)}) %all-to-all-start.1) | async-done | bytes 524320 | tf_op jit(solution)/shard_map/all_to_all | solution.py:358
  58.8 0.0 copy-start.1
  58.8 0.8 %copy-done.1 = f32[8,128,128]{2,1,0:T(8,128)} copy-done((f32[8,128,128]{2,1,0:T(8,128)}, f32[8,128,128]{2,1,0:T(8,128)S(1)}, u32[]{:S(2)}) %copy-start.1) | copy-done | bytes 524312
  59.6 12.5 %solve.1 = f32[16,2048]{1,0:T(8,128)} custom-call(f32[8,128,128]{2,1,0:T(8,128)} %copy-done.1, s32[1]{0:T(128)S(6)} %copy.11.order_ref, f32[16,2048]{1,0:T(8,128)} %science_ref.3, bf16[512,2048]{1,0:T(8,128)(2,1)} %get-tuple-element.14.basis_any_ref), custom_call_target="tpu_custom_call" | custom-call | tf_op jit(solution)/shard_map/solve/pallas_call | solution.py:360
Async XLA Ops:
  6.2 26.5 %all-to-all-start = ((f32[32,40,128]{2,1,0:T(8,128)}), f32[32,40,128]{2,1,0:T(8,128)S(1)}, u32[]{:S(2)}, u32[]{:S(2)}) async-start(f32[32,40,128]{2,1,0:T(8,128)} %pack.1), calls=%async_computation | async-start | bytes 1310720 | tf_op jit(solution)/shard_map/all_to_all | solution.py:327
  32.7 0.8 %copy-start = (f32[32,40,128]{2,1,0:T(8,128)}, f32[32,40,128]{2,1,0:T(8,128)S(1)}, u32[]{:S(2)}) copy-start(f32[32,40,128]{2,1,0:T(8,128)S(1)} %all-to-all-done.arrived_ref) | copy-start | bytes 1966084
  41.1 17.7 %all-to-all-start.1 = ((f32[8,128,128]{2,1,0:T(8,128)}), f32[8,128,128]{2,1,0:T(8,128)S(1)}, u32[]{:S(2)}, u32[]{:S(2)}) async-start(f32[8,128,128]{2,1,0:T(8,128)} %get-tuple-element.13), calls=%async_computation.1 | async-start | bytes 1048576 | tf_op jit(solution)/shard_map/all_to_all | solution.py:358
  58.8 0.8 %copy-start.1 = (f32[8,128,128]{2,1,0:T(8,128)}, f32[8,128,128]{2,1,0:T(8,128)S(1)}, u32[]{:S(2)}) copy-start(f32[8,128,128]{2,1,0:T(8,128)S(1)} %all-to-all-done.1.moment_ref) | copy-start | bytes 1572868

commit v2 on v1

v2 whole, which is shorter than its diff:
```python
import math

import jax
import jax.numpy as jnp
from jax import lax
from jax.experimental import pallas as pl
from jax.experimental.pallas import tpu as pltpu
from jax.sharding import PartitionSpec as P

H = 11
CM = 128
TW = 2304
LANES = 128
SLOTS = 32

gauss_sigmas = (0.7, 1.5, 3.0)
poly_degrees = (4, 2, 2)
mono_degrees = (0, 1, 1, 2, 2, 2)
mono_powers = ((0, 0), (1, 0), (0, 1), (2, 0), (1, 1), (0, 2))
ridge_weight = 0.05

filters = [(g, n) for g, top in enumerate(poly_degrees) for n in range(top + 1)]
basis_list = [
    (g, i, j) for g, top in enumerate(poly_degrees) for i in range(top + 1) for j in range(top + 1 - i)
]
NB = len(basis_list)
NF = len(filters)
ONE = NB
SCI = NB + 1
moment_keys = [(a, c) for c in range(5) for a in range(5 - c)]
NQ = len(mono_powers)


def envelope_norm(sigma):
    return sum(math.exp(-a * a / (2.0 * sigma * sigma)) for a in range(-H, H + 1))


def iota(shape, dim):
    return lax.broadcasted_iota(jnp.int32, shape, dim)


def split_two(value):
    high = value.astype(jnp.bfloat16)
    low = (value - high.astype(jnp.float32)).astype(jnp.bfloat16)
    return high, low


def pack_kernel(store_hbm_ref, source_hbm_ref, slot_hbm_ref, out_ref, store_ref, source_ref, slot_ref, sems):
    pairs = ((source_hbm_ref, source_ref), (slot_hbm_ref, slot_ref), (store_hbm_ref, store_ref))
    copies = [pltpu.make_async_copy(here, there, sems.at[n]) for n, (here, there) in enumerate(pairs)]
    for copy in copies:
        copy.start()
    me = lax.axis_index("ccd") * lax.axis_size("strip") + lax.axis_index("strip")
    copies[0].wait()
    copies[1].wait()
    source = source_ref[...]
    slots = jnp.sum(jnp.where(source == me, slot_ref[...], 0), axis=0, keepdims=True)
    copies[2].wait()
    for strip in range(out_ref.shape[0]):
        out_ref[strip] = store_ref[slots[0, strip]]


def window_kernel(arrived_ref, owner_ref, shift_ref, window_ref, partner_ref, other_ref):
    even = lax.rem(lax.axis_index("strip"), 2) == 0
    tiles = owner_ref.shape[0]
    rows = arrived_ref.shape[1]
    count = window_ref.shape[1] // LANES
    start = CM - H + shift_ref[0]
    skip = start >= LANES
    offset = start - jnp.where(skip, LANES, 0)
    turn = lax.rem(LANES - offset, LANES)
    stays = iota((rows, LANES), 1) < LANES - offset
    owners = owner_ref[...]
    owners = [owners[t, 0] for t in range(tiles)]
    turned = []
    for w in range(count + 1):
        owner = jnp.where(skip, owners[min(w + 1, tiles - 1)], owners[w])
        turned.append(pltpu.roll(arrived_ref[owner], turn, 1))
    for w in range(count):
        tile = jnp.where(stays, turned[w], turned[w + 1])
        window_ref[:, w * LANES : (w + 1) * LANES] = tile
        last, first = tile[rows - H :], tile[:H]
        partner_ref[w * H : (w + 1) * H, :] = jnp.where(even, last, first)
        other_ref[w * H : (w + 1) * H, :] = jnp.where(even, first, last)
    spare = partner_ref.shape[0] - count * H
    partner_ref[count * H :, :] = jnp.zeros((spare, LANES), jnp.float32)
    other_ref[count * H :, :] = jnp.zeros((spare, LANES), jnp.float32)


def table_kernel(source_ref, owner_ref, horizontal_high_ref, horizontal_low_ref, vertical_ref, *, rows, halo):
    me = lax.axis_index("ccd") * lax.axis_size("strip") + lax.axis_index("strip")
    source = source_ref[...]
    owner = jnp.sum(jnp.where(iota(source.shape, 1) == me, source, 0), axis=1, keepdims=True)
    owner_ref[...] = jnp.broadcast_to(owner, owner_ref.shape)
    offset = (iota((2 * LANES, LANES), 0) - iota((2 * LANES, LANES), 1) - H).astype(jnp.float32)
    inside = jnp.abs(offset) <= H
    for f, (g, n) in enumerate(filters):
        sigma = gauss_sigmas[g]
        tap = jnp.exp(-offset * offset / (2.0 * sigma * sigma)) * (1.0 / envelope_norm(sigma))
        for _ in range(n):
            tap = tap * (offset * (1.0 / sigma))
        tap = jnp.where(inside, tap, 0.0)
        tap_high, tap_low = split_two(tap)
        horizontal_high_ref[:, f * LANES : (f + 1) * LANES] = tap_high
        horizontal_low_ref[:, f * LANES : (f + 1) * LANES] = tap_low
    width = vertical_ref.shape[1]
    slot = iota((SLOTS, width), 0)
    column = iota((SLOTS, width), 1)
    wanted = jnp.full((SLOTS, width), -1, jnp.int32)
    degree = jnp.zeros((SLOTS, width), jnp.int32)
    scale = jnp.ones((SLOTS, width), jnp.float32)
    weight = jnp.zeros((SLOTS, width), jnp.float32)
    for b, (g, i, j) in enumerate(basis_list):
        here = slot == b
        wanted = jnp.where(here, filters.index((g, i)), wanted)
        degree = jnp.where(here, j, degree)
        scale = jnp.where(here, 1.0 / gauss_sigmas[g], scale)
        weight = jnp.where(here, 1.0 / envelope_norm(gauss_sigmas[g]), weight)
    own = column - wanted * rows
    outside = column - NF * rows - wanted * halo
    is_own = (own >= 0) & (own < rows)
    is_above = (outside >= 0) & (outside < H)
    is_below = (outside >= H) & (outside < 2 * H)
    is_own = is_own & (column < NF * rows)
    row_in = jnp.where(is_own, own + H, jnp.where(is_below, outside + rows, outside))
    matched = is_own | ((column >= NF * rows) & (is_above | is_below))
    for r in range(rows):
        a = row_in - (r + H)
        z = a.astype(jnp.float32) * scale
        tap = jnp.exp(-0.5 * z * z) * weight
        square = z * z
        power = jnp.where(degree == 1, z, jnp.where(degree == 2, square, 1.0))
        power = jnp.where(degree == 3, square * z, jnp.where(degree == 4, square * square, power))
        keep = matched & (jnp.abs(a) <= H)
        vertical_ref[r * SLOTS : (r + 1) * SLOTS, :] = jnp.where(keep, tap * power, 0.0).astype(jnp.bfloat16)


def wide_tile(value):
    return jnp.concatenate([value, jnp.zeros((value.shape[0], LANES - value.shape[1]), value.dtype)], axis=1)


def turn_lanes(value, by):
    if value.shape[1] < LANES:
        value = wide_tile(value)
    return pltpu.roll(value, by % LANES, 1) if by % LANES else value


def u_row(cols):
    return 2.0 * (iota((1, cols), 1).astype(jnp.float32) + 0.5) / cols - 1.0


def filter_rows(padded, high_ref, low_ref, filtered_ref, out_ref):
    count = padded.shape[0]
    blocks = filtered_ref.shape[0] // count
    window = [split_two(padded[:, w * LANES : (w + 1) * LANES]) for w in range(blocks + 1)]
    left = []
    for w in range(blocks):
        (h0, l0), (h1, l1) = window[w], window[w + 1]
        left.append(jnp.concatenate([h0, h1, l0, l1, h0, h1], axis=1))
    left = jnp.concatenate(left, axis=0)
    right = jnp.concatenate([high_ref[...], high_ref[...], low_ref[...]], axis=0)
    filtered_ref[...] = jnp.dot(left, right, preferred_element_type=jnp.float32)
    for w in range(blocks):
        out_ref[:, w * LANES : (w + 1) * LANES] = jnp.concatenate(
            [filtered_ref[w * count : (w + 1) * count, f * LANES : (f + 1) * LANES] for f in range(NF)],
            axis=0,
        ).astype(jnp.bfloat16)


def own_kernel(window_ref, high_ref, low_ref, out_ref, filtered_ref):
    filter_rows(window_ref[...], high_ref, low_ref, filtered_ref, out_ref)


def basis_kernel(
    own_ref, partner_ref, other_ref, science_hbm_ref, high_ref, low_ref, vertical_ref,
    basis_ref, moment_out_ref,
    padded_ref, filtered_ref, outside_ref, science_ref, moment_ref, sems,
):
    strip_count = lax.axis_size("strip")
    strip = lax.axis_index("strip")
    rows, cols = science_ref.shape
    blocks = cols // LANES
    science_copy = pltpu.make_async_copy(science_hbm_ref, science_ref, sems.at[0])
    science_copy.start()
    even = lax.rem(strip, 2) == 0
    padded_ref[2 * H :, :] = jnp.zeros((padded_ref.shape[0] - 2 * H, padded_ref.shape[1]), jnp.float32)
    for w in range(blocks + 1):
        at = slice(w * LANES, (w + 1) * LANES)
        partner, other = partner_ref[w * H : (w + 1) * H, :], other_ref[w * H : (w + 1) * H, :]
        padded_ref[0:H, at] = jnp.where(even, other, partner)
        padded_ref[H : 2 * H, at] = jnp.where(even, partner, other)
    filter_rows(padded_ref[...], high_ref, low_ref, filtered_ref, outside_ref)

    eighth = iota((8, 2 * LANES), 0)
    science_copy.wait()
    for pair in range(blocks // 2):
        at = slice(pair * 2 * LANES, (pair + 1) * 2 * LANES)
        block = jnp.dot(
            vertical_ref[...],
            jnp.concatenate([own_ref[:, at], outside_ref[:, at]], axis=0),
            preferred_element_type=jnp.float32,
        )
        parts = []
        for r in range(rows):
            last = block[(r + 1) * SLOTS - 8 : (r + 1) * SLOTS]
            last = jnp.where(eighth == ONE % 8, 1.0, jnp.where(eighth == SCI % 8, science_ref[r : r + 1, at], last))
            parts += [block[r * SLOTS : (r + 1) * SLOTS - 8], last]
        basis_ref[:, at] = jnp.concatenate(parts, axis=0).astype(jnp.bfloat16)
    u = u_row(cols)
    square = u * u
    totals = [None] * 5
    for r in range(rows):
        here = basis_ref[r * SLOTS : (r + 1) * SLOTS, :]
        wide = here.astype(jnp.float32)
        design = jnp.concatenate(
            [here, (wide * u).astype(jnp.bfloat16), (wide * square).astype(jnp.bfloat16)], axis=0
        )
        product = lax.dot_general(
            design, design, (((1,), (1,)), ((), ())), preferred_element_type=jnp.float32
        )
        v = 2.0 * ((strip * rows + r).astype(jnp.float32) + 0.5) / (rows * strip_count) - 1.0
        for c in range(5):
            totals[c] = product if totals[c] is None else totals[c] + product
            product = product * v
    half = SLOTS // 2
    row = iota((half, LANES), 0)
    lane = iota((half, LANES), 1)
    chunks = [jnp.zeros((half, LANES), jnp.float32) for _ in range(moment_ref.shape[0] // half)]
    for at, (a, c) in enumerate(moment_keys):
        first, second = (a, 0) if a < 3 else (a - 2, 2)
        group = at % 4 * SLOTS
        top = totals[c][first * SLOTS : first * SLOTS + half, :]
        bottom = totals[c][first * SLOTS + half : (first + 1) * SLOTS, :]
        by = group - second * SLOTS
        corner = jnp.where(lane - group - half <= row, turn_lanes(top, by + half), turn_lanes(bottom, by + 1))
        both = jnp.where(lane - group < half, turn_lanes(bottom, by), corner)
        chunks[at // 4] = jnp.where(lane // SLOTS == at % 4, both, chunks[at // 4])
    for p, chunk in enumerate(chunks):
        moment_ref[p * half : (p + 1) * half, :] = chunk
    sends = []
    for k in range(moment_out_ref.shape[0]):
        sends.append(pltpu.make_async_copy(moment_ref, moment_out_ref.at[k], sems.at[1 + k]))
        sends[k].start()
    for send in sends:
        send.wait()


def solve_kernel(
    moment_ref, order_ref, science_hbm_ref, basis_ref, out_ref,
    system_ref, science_ref, sem,
):
    strip_count = lax.axis_size("strip")
    strip = lax.axis_index("strip")
    rows, cols = science_ref.shape
    copy = pltpu.make_async_copy(science_hbm_ref, science_ref, sem)
    copy.start()
    order = order_ref[0]
    total = moment_ref[0]
    for k in range(1, moment_ref.shape[0]):
        total = total + moment_ref[k]
    half = SLOTS // 2
    across = jnp.transpose(jnp.concatenate([total, jnp.zeros((LANES - total.shape[0], LANES), jnp.float32)], axis=0))
    next_across = pltpu.roll(across, LANES - 1, 0)
    half_row = iota((half, LANES), 0)
    half_lane = iota((half, LANES), 1)
    pieces = {}
    for at, key in enumerate(moment_keys):
        here = total[at // 4 * half : (at // 4 + 1) * half, :]
        group, place = at % 4 * SLOTS, at // 4 * half
        first = across[group : group + half, :]
        second = across[group + half : group + SLOTS, :]
        shifted = next_across[group + half : group + SLOTS, :]
        corner = jnp.where(
            half_lane <= half_row, turn_lanes(here, -group - half), turn_lanes(second, -place)
        )
        top = jnp.where(half_lane < half, corner, turn_lanes(first, half - place))
        corner = jnp.where(
            half_lane - half >= half_row, turn_lanes(here, -group - 1), turn_lanes(shifted, half - place)
        )
        bottom = jnp.where(half_lane < half, turn_lanes(here, -group), corner)
        pieces[key] = jnp.concatenate([top, bottom], axis=0)
    lane = iota((SLOTS, LANES), 1)
    lane_slot = lane & (SLOTS - 1)
    lane_group = lane // SLOTS
    row_slot = iota((SLOTS, LANES), 0)

    def active(slot, q):
        return ((slot < NB) & (mono_degrees[q] <= order)) | (slot == ONE)

    def moved(key, to_lane, from_lane):
        return turn_lanes(pieces[key], to_lane - from_lane)

    for q, (aq, cq) in enumerate(mono_powers):
        tiles = [jnp.zeros((SLOTS, LANES), jnp.float32) for _ in range(2)]
        for k, (ak, ck) in enumerate(mono_powers):
            keep = (lane_group == k % 4) & active(lane_slot, k)
            tiles[k // 4] = jnp.where(keep, moved((aq + ak, cq + ck), (k % 4) * SLOTS, 0), tiles[k // 4])
        tiles[1] = jnp.where(lane == 2 * SLOTS, moved((aq, cq), 2 * SLOTS, SCI), tiles[1])
        row_on = active(row_slot, q)
        for side in range(2):
            tile = jnp.where(row_on, tiles[side], 0.0)
            if q // 4 == side:
                diagonal = lane == row_slot + (q % 4) * SLOTS
                weight = jnp.where(row_on, tile, 1.0) * (1.0 + ridge_weight)
                tile = jnp.where(diagonal, weight, tile)
            system_ref[q * SLOTS : (q + 1) * SLOTS, side * LANES : (side + 1) * LANES] = tile

    groups = [
        [system_ref[8 * i : 8 * i + 8, side * LANES : (side + 1) * LANES] for side in range(2)]
        for i in range(NQ * SLOTS // 8)
    ]
    row8 = iota((8, LANES), 0)

    def column(value, at):
        return jnp.broadcast_to(value[:, at : at + 1], (8, LANES))

    def row_of(value, at):
        return jnp.broadcast_to(value[at : at + 1, :], (8, LANES))

    per = SLOTS // 8
    for q in range(NQ):
        side, start = divmod(q * SLOTS, LANES)
        inner = list(range(q * per, (q + 1) * per))
        for block in inner:
            first = 8 * block % LANES
            count = min(8, NB + 1 - 8 * block % SLOTS)
            panel = [column(groups[block][side], first + j) for j in range(count)] + groups[block][side:]
            for k in range(count):
                inverse = 1.0 / row_of(panel[k], k)
                pivot = row8 == k
                factor = jnp.where(pivot, inverse, -panel[k] * inverse)
                for j in range(k + 1, len(panel)):
                    panel[j] = jnp.where(pivot, 0.0, panel[j]) + factor * row_of(panel[j], k)
            ready = panel[count:]
            spread_rows = [[row_of(tile, j) for j in range(count)] for tile in ready]
            groups[block][side:] = ready
            for i in inner:
                if i != block:
                    factors = [column(groups[i][side], first + j) for j in range(count)]
                    for t in range(side, 2):
                        for j in range(count):
                            groups[i][t] = groups[i][t] - factors[j] * spread_rows[t - side][j]
        ahead = list(range((q + 1) * per, (q + 2) * per)) if q + 1 < NQ else []
        for i in ahead:
            factors = [column(groups[i][side], start + j) for j in range(NB + 1)]
            for t in range(side, 2):
                for j in range(NB + 1):
                    groups[i][t] = groups[i][t] - factors[j] * row_of(groups[inner[j // 8]][t], j % 8)
        rest = [i for i in range(len(groups)) if i not in inner and i not in ahead]
        left = jnp.concatenate([groups[i][side] for i in rest], axis=0)
        right = jnp.concatenate([jnp.concatenate([groups[i][t] for i in inner], axis=0) for t in range(side, 2)], axis=1)
        padding = [jnp.zeros((n, right.shape[1]), jnp.float32) for n in (start, LANES - start - SLOTS)]
        right = jnp.concatenate([x for x in (padding[0], right, padding[1]) if x.shape[0]], axis=0)
        change = jnp.dot(left, right, precision=lax.Precision.HIGHEST, preferred_element_type=jnp.float32)
        for n, i in enumerate(rest):
            for t in range(side, 2):
                groups[i][t] = groups[i][t] - change[8 * n : 8 * n + 8, (t - side) * LANES : (t - side + 1) * LANES]
    solved = jnp.concatenate([group[1][:, 2 * SLOTS : 2 * SLOTS + 1] for group in groups], axis=0)
    turned = []
    for q in range(NQ):
        part = solved[q * SLOTS : (q + 1) * SLOTS]
        part = jnp.broadcast_to(jnp.concatenate([part] * (LANES // SLOTS), axis=0), (LANES, LANES))
        turned.append(jnp.transpose(part)[0:rows, :])
    row = iota((rows, LANES), 0)
    v = 2.0 * ((strip * rows + row).astype(jnp.float32) + 0.5) / (rows * strip_count) - 1.0
    group = iota((rows, LANES), 1) // SLOTS
    weights = [jnp.zeros((rows, LANES), jnp.float32) for _ in range(3)]
    for q, (a, c) in enumerate(mono_powers):
        weights[a] = weights[a] + turned[q] * (v * v if c == 2 else v if c else jnp.ones_like(v))
    spread = jnp.concatenate(
        [
            jnp.concatenate(
                [jnp.where(group + m * (LANES // SLOTS) == row, w, 0.0) for m in range(rows * SLOTS // LANES)],
                axis=1,
            )
            for w in weights
        ],
        axis=0,
    )
    spread_high, spread_low = split_two(spread)
    spread = jnp.concatenate([spread_high, spread_low], axis=0)
    copy.wait()
    sums = jnp.dot(spread, basis_ref[...], preferred_element_type=jnp.float32)
    u = u_row(cols)
    model = [sums[a * rows : (a + 1) * rows] + sums[(a + 3) * rows : (a + 4) * rows] for a in range(3)]
    out_ref[...] = science_ref[...] - (model[0] + u * (model[1] + u * model[2]))


def body(tile_store, tile_source, tile_slot, shift_cols, spatial_order, science):
    strip_count = lax.axis_size("strip")
    device_count = lax.axis_size("ccd") * strip_count
    rows, cols = science.shape
    halo = -(-2 * H // 8) * 8
    vmem = pl.BlockSpec(memory_space=pltpu.VMEM)
    smem = pl.BlockSpec(memory_space=pltpu.SMEM)
    hbm = pl.BlockSpec(memory_space=pltpu.HBM)

    def outside(value):
        return pltpu.with_memory_space_constraint(value, pltpu.HBM)

    def kept(value):
        return pltpu.with_memory_space_constraint(value, pltpu.VMEM)

    tile_store, source, slot, science = map(outside, (tile_store, tile_source.T, tile_slot.T, science))

    def params(mib):
        return pltpu.CompilerParams(vmem_limit_bytes=mib * 1024 * 1024)

    outgoing = pl.pallas_call(
        pack_kernel,
        out_shape=jax.ShapeDtypeStruct((device_count,) + tile_store.shape[1:], jnp.float32),
        in_specs=[hbm, hbm, hbm],
        out_specs=vmem,
        scratch_shapes=[
            pltpu.VMEM(tile_store.shape, jnp.float32),
            pltpu.VMEM(source.shape, jnp.int32),
            pltpu.VMEM(slot.shape, jnp.int32),
            pltpu.SemaphoreType.DMA((3,)),
        ],
        compiler_params=params(60),
        name="pack",
    )(tile_store, source, slot)
    arrived = lax.all_to_all(outgoing, ("ccd", "strip"), split_axis=0, concat_axis=0, tiled=True)
    owner, taps_high, taps_low, vertical = pl.pallas_call(
        lambda *refs: table_kernel(*refs, rows=rows, halo=halo),
        out_shape=(
            pltpu.VMEM((tile_source.shape[1], LANES), jnp.int32),
            pltpu.VMEM((2 * LANES, NF * LANES), jnp.bfloat16),
            pltpu.VMEM((2 * LANES, NF * LANES), jnp.bfloat16),
            pltpu.VMEM((rows * SLOTS, NF * (rows + halo)), jnp.bfloat16),
        ),
        in_specs=[vmem],
        out_specs=(vmem, vmem, vmem, vmem),
        compiler_params=params(16),
        name="tables",
        cost_estimate=pl.CostEstimate(flops=10_000_000, bytes_accessed=2_000_000, transcendentals=1_000_000),
    )(source)
    count = cols // LANES + 1
    edge = -(-count * H // 8) * 8
    window, to_partner, to_other = pl.pallas_call(
        window_kernel,
        out_shape=(
            jax.ShapeDtypeStruct((rows, count * LANES), jnp.float32),
            jax.ShapeDtypeStruct((edge, LANES), jnp.float32),
            jax.ShapeDtypeStruct((edge, LANES), jnp.float32),
        ),
        in_specs=[vmem, vmem, smem],
        out_specs=(vmem, vmem, vmem),
        compiler_params=params(16),
        name="window",
    )(arrived, kept(owner), shift_cols)

    def swap(value, start):
        pairs = [(i, i + 1) for i in range(start, strip_count - 1, 2)]
        return lax.ppermute(value, "strip", pairs + [(j, i) for i, j in pairs])

    from_other = swap(to_other, 1)
    from_partner = swap(to_partner, 0)

    filtered_own = pl.pallas_call(
        own_kernel,
        out_shape=pltpu.VMEM((NF * rows, cols), jnp.bfloat16),
        in_specs=[vmem, vmem, vmem],
        out_specs=vmem,
        scratch_shapes=[pltpu.VMEM((cols // LANES * rows, NF * LANES), jnp.float32)],
        compiler_params=params(16),
        name="own",
        cost_estimate=pl.CostEstimate(flops=600_000_000, bytes_accessed=3_000_000, transcendentals=0),
    )(window, kept(taps_high), kept(taps_low))
    half = SLOTS // 2
    packed = -(-len(moment_keys) // 4) * half
    basis, moments = pl.pallas_call(
        basis_kernel,
        out_shape=(
            pltpu.VMEM((rows * SLOTS, cols), jnp.bfloat16),
            pltpu.HBM((strip_count, packed, LANES), jnp.float32),
        ),
        in_specs=[vmem, vmem, vmem, hbm, vmem, vmem, vmem],
        out_specs=(vmem, hbm),
        scratch_shapes=[
            pltpu.VMEM((halo, count * LANES), jnp.float32),
            pltpu.VMEM((cols // LANES * halo, NF * LANES), jnp.float32),
            pltpu.VMEM((NF * halo, cols), jnp.bfloat16),
            pltpu.VMEM((rows, cols), jnp.float32),
            pltpu.VMEM((packed, LANES), jnp.float32),
            pltpu.SemaphoreType.DMA((1 + strip_count,)),
        ],
        compiler_params=params(24),
        name="basis",
    )(kept(filtered_own), from_partner, from_other, science, kept(taps_high), kept(taps_low), kept(vertical))
    gathered = lax.all_to_all(moments, "strip", split_axis=0, concat_axis=0, tiled=True)

    return pl.pallas_call(
        solve_kernel,
        out_shape=jax.ShapeDtypeStruct((rows, cols), jnp.float32),
        in_specs=[vmem, smem, hbm, vmem],
        out_specs=vmem,
        scratch_shapes=[
            pltpu.VMEM((NQ * SLOTS, 2 * LANES), jnp.float32),
            pltpu.VMEM((rows, cols), jnp.float32),
            pltpu.SemaphoreType.DMA,
        ],
        compiler_params=params(16),
        name="solve",
    )(gathered, spatial_order, science, kept(basis))


def solution(mesh):
    placed = (
        P(("ccd", "strip"), None, None),
        P(),
        P(),
        P("ccd"),
        P("ccd"),
        P(("ccd", "strip"), None),
    )
    return jax.shard_map(
        body, mesh=mesh, in_specs=placed, out_specs=P(("ccd", "strip"), None), check_vma=False
    )
```

time: 72.6 us -> 53.8 us (0.74)
  waiting for transfers between devices: 29.9 us -> 16.6 us
  Pallas kernels: 25.7 us -> 19 us
  starting transfers between devices: 10.8 us -> 15.6 us
  local copies, waits for them, and re-layouts: 4.4 us -> 0.79 us
    all_to_all x1, waiting for transfers between devices: 16.3 us -> 6.87 us  [body(): lax.all_to_all(outgoing, ('ccd', 'strip'), split_axis=0, concat_axis=0, t...]
    all_to_all x1, waiting for transfers between devices: 13.6 us -> 7.57 us  [body(): lax.all_to_all(moments, 'strip', split_axis=0, concat_axis=0, tiled=True)]
    pallas_call x1, Pallas kernels: 12.5 us -> 8.42 us  [body(): pl.pallas_call(solve_kernel, out_shape=jax.ShapeDtypeStruct((rows, cols),...]
    unnamed x6 -> x4, local copies, waits for them, and re-layouts: 4.4 us -> 0.79 us
    all_to_all x1, starting transfers between devices: 3.5 us -> 6.53 us  [body(): lax.all_to_all(moments, 'strip', split_axis=0, concat_axis=0, tiled=True)]
    ppermute x0 -> x2, waiting for transfers between devices: none -> 2.15 us  [swap(): return lax.ppermute(value, 'strip', pairs + [(j, i) for i, j in pairs])]
    ppermute x0 -> x2, starting transfers between devices: none -> 1.74 us  [swap(): return lax.ppermute(value, 'strip', pairs + [(j, i) for i, j in pairs])]
    pallas_call x1, Pallas kernels: 3.42 us -> 1.8 us  [body(): pl.pallas_call(pack_kernel, out_shape=jax.ShapeDtypeStruct((device_count,...]
  transfers between devices with their start and end apart: 2 -> 4, of which waited for: 2 -> 3; matrix products, arithmetic and copies ran while one was open for 0% -> 0% of each run, Pallas kernels for 3% -> 6%
where the time goes in v2:
time: 53.8 us; the launch traced here: 53.3 us
  Pallas kernels  19 us (35%)
  waiting for transfers between devices  16.6 us (31%)
  starting transfers between devices  15.6 us (29%)
  between operations  1.36 us (3%)
  local copies, waits for them, and re-layouts  0.79 us (1%)
    pallas_call x1, Pallas kernels, body(): pl.pallas_call(solve_kernel, out_shape=jax.ShapeDtypeStruct((rows, cols),...  8.42 us
    all_to_all x1, waiting for transfers between devices, body(): lax.all_to_all(moments, 'strip', split_axis=0, concat_axis=0, tiled=True)  7.57 us
    all_to_all x1, starting transfers between devices, body(): lax.all_to_all(outgoing, ('ccd', 'strip'), split_axis=0, concat_axis=0, t...  7.3 us
    all_to_all x1, waiting for transfers between devices, body(): lax.all_to_all(outgoing, ('ccd', 'strip'), split_axis=0, concat_axis=0, t...  6.87 us
    all_to_all x1, starting transfers between devices, body(): lax.all_to_all(moments, 'strip', split_axis=0, concat_axis=0, tiled=True)  6.53 us
    pallas_call x1, Pallas kernels, body(): pl.pallas_call(basis_kernel, out_shape=(pltpu.VMEM((rows * SLOTS, cols),...  5.55 us
    pallas_call x1, Pallas kernels, body(): pl.pallas_call(lambda *refs: table_kernel(*refs, rows=rows, halo=halo), o...  2.34 us
    ppermute x2, waiting for transfers between devices, swap(): return lax.ppermute(value, 'strip', pairs + [(j, i) for i, j in pairs])  2.15 us
  transfers between devices with their start and end apart: 4, of which 3 were waited for; matrix products, arithmetic and copies ran while one was open for 0% of the time, Pallas kernels for 6%

profile of v2, /device:TPU:0, one launch (start us, length us, event | category | flops | bytes accessed | tf_op | source)
XLA Modules:
  0.0 53.3 jit_solution(16874904108315921741)
XLA Ops:
  0.0 1.8 %pack.1 = f32[32,16,128]{2,1,0:T(8,128)} custom-call(f32[18,16,128]{2,1,0:T(8,128)} %store_hbm_ref.1, s32[18,32]{1,0:T(8,128)} %bitcast.3, s32[18,32]{1,0:T(8,128)} %bitcast.2), custom_call_target="tpu_custom_call" | custom-call | tf_op jit(solution)/shard_map/pack/pallas_call | solution.py:409
  1.8 7.3 %all-to-all-start = ((f32[32,16,128]{2,1,0:T(8,128)}), f32[32,16,128]{2,1,0:T(8,128)S(1)}, u32[]{:S(2)}, u32[]{:S(2)}) async-start(f32[32,16,128]{2,1,0:T(8,128)} %pack.1), calls=%async_computation | async-start | bytes 524288 | tf_op jit(solution)/shard_map/all_to_all | solution.py:423
  9.8 2.3 %tables.1 = (s32[18,128]{1,0:T(8,128)S(1)}, bf16[256,1408]{1,0:T(8,128)(2,1)S(1)}, bf16[256,1408]{1,0:T(8,128)(2,1)S(1)}, bf16[512,440]{1,0:T(8,128)(2,1)S(1)}) custom-call(s32[18,32]{1,0:T(8,128)} %bitcast.4), custom_call_target="tpu_custom_call" | custom-call | flops 10000000 | bytes 2000000 | tf_op jit(solution)/shard_map/tables/pallas_call | solution.py:424
  12.1 0.0 copy-start
  12.1 0.8 %copy-done = bf16[512,440]{1,0:T(8,128)(2,1)} copy-done((bf16[512,440]{1,0:T(8,128)(2,1)}, bf16[512,440]{1,0:T(8,128)(2,1)S(1)}, u32[]{:S(2)}) %copy-start) | copy-done | bytes 450584
  12.9 6.9 %all-to-all-done.arrived_ref = f32[32,16,128]{2,1,0:T(8,128)S(1)} async-done(((f32[32,16,128]{2,1,0:T(8,128)}), f32[32,16,128]{2,1,0:T(8,128)S(1)}, u32[]{:S(2)}, u32[]{:S(2)}) %all-to-all-start) | async-done | bytes 262176 | tf_op jit(solution)/shard_map/all_to_all | solution.py:423
  19.8 0.0 copy-start.1
  19.8 0.1 window.1
  19.9 1.1 %collective-permute-start = (f32[192,128]{1,0:T(8,128)S(1)}, f32[192,128]{1,0:T(8,128)S(1)}, u32[]{:S(2)}, u32[]{:S(2)}) collective-permute-start(f32[192,128]{1,0:T(8,128)S(1)} %get-tuple-element.18), channel_id=1, source_target_pairs={{0,1},{2,3},{4,5},{6,7},{1,0},{3,2},{5,4},{7,6},{8,9},{10,11},{12,... | collective-permute-start | bytes 294920 | tf_op jit(solution)/shard_map/ppermute | solution.py:455
  21.0 0.7 %collective-permute-start.1 = (f32[192,128]{1,0:T(8,128)S(1)}, f32[192,128]{1,0:T(8,128)S(1)}, u32[]{:S(2)}, u32[]{:S(2)}) collective-permute-start(f32[192,128]{1,0:T(8,128)S(1)} %get-tuple-element.19), channel_id=1, source_target_pairs={{1,2},{3,4},{5,6},{2,1},{4,3},{6,5},{9,10},{11,12},{13,14},{10,9},... | collective-permute-start | bytes 294920 | tf_op jit(solution)/shard_map/ppermute | solution.py:455
  21.7 0.8 %own.1.own_ref = bf16[176,2048]{1,0:T(8,128)(2,1)S(1)} custom-call(f32[16,2176]{1,0:T(8,128)S(1)} %get-tuple-element.15.window_ref, bf16[256,1408]{1,0:T(8,128)(2,1)S(1)} %get-tuple-element.16.high_ref, bf16[256,1408]{1,0:T(8,128)(2,1)S(1)} %get-tuple-element.17.low_ref), custom_call_target="tpu_custom_call" | custom-call | flops 600000000 | bytes 3000000 | tf_op jit(solution)/shard_map/own/pallas_call | solution.py:460
  22.5 2.1 %collective-permute-done.partner_ref = f32[192,128]{1,0:T(8,128)S(1)} collective-permute-done((f32[192,128]{1,0:T(8,128)S(1)}, f32[192,128]{1,0:T(8,128)S(1)}, u32[]{:S(2)}, u32[]{:S(2)}) %collective-permute-start) | collective-permute-done | bytes 98336 | tf_op jit(solution)/shard_map/ppermute | solution.py:455
  24.6 0.0 collective-permute-done.1.other_ref
  24.6 0.0 copy-done.1
  24.6 5.5 %basis.1 = (bf16[512,2048]{1,0:T(8,128)(2,1)S(1)}, f32[8,64,128]{2,1,0:T(8,128)}) custom-call(bf16[176,2048]{1,0:T(8,128)(2,1)S(1)} %own.1.own_ref, f32[192,128]{1,0:T(8,128)S(1)} %collective-permute-done.partner_ref, f32[192,128]{1,0:T(8,128)S(1)} %collective-permute-done.1.other_ref, f32[16,2048]{1,0:T(8,128)} %science_hbm_ref.3, ...), custom_call_target="tpu_custom_call" | custom-call | tf_op jit(solution)/shard_map/basis/pallas_call | solution.py:472
  30.2 6.5 %all-to-all-start.1 = ((f32[8,64,128]{2,1,0:T(8,128)}), f32[8,64,128]{2,1,0:T(8,128)S(1)}, u32[]{:S(2)}, u32[]{:S(2)}) async-start(f32[8,64,128]{2,1,0:T(8,128)} %get-tuple-element.21), calls=%async_computation.1 | async-start | bytes 524288 | tf_op jit(solution)/shard_map/all_to_all | solution.py:491
  37.3 7.6 %all-to-all-done.1.moment_ref = f32[8,64,128]{2,1,0:T(8,128)S(1)} async-done(((f32[8,64,128]{2,1,0:T(8,128)}), f32[8,64,128]{2,1,0:T(8,128)S(1)}, u32[]{:S(2)}, u32[]{:S(2)}) %all-to-all-start.1) | async-done | bytes 262176 | tf_op jit(solution)/shard_map/all_to_all | solution.py:491
  44.9 8.4 %solve.1 = f32[16,2048]{1,0:T(8,128)} custom-call(f32[8,64,128]{2,1,0:T(8,128)S(1)} %all-to-all-done.1.moment_ref, s32[1]{0:T(128)S(6)} %copy.8.order_ref, f32[16,2048]{1,0:T(8,128)} %science_hbm_ref.3, bf16[512,2048]{1,0:T(8,128)(2,1)S(1)} %get-tuple-element.22.basis_ref), custom_call_target="tpu_custom_call" | custom-call | tf_op jit(solution)/shard_map/solve/pallas_call | solution.py:493
Async XLA Ops:
  1.8 18.0 %all-to-all-start = ((f32[32,16,128]{2,1,0:T(8,128)}), f32[32,16,128]{2,1,0:T(8,128)S(1)}, u32[]{:S(2)}, u32[]{:S(2)}) async-start(f32[32,16,128]{2,1,0:T(8,128)} %pack.1), calls=%async_computation | async-start | bytes 524288 | tf_op jit(solution)/shard_map/all_to_all | solution.py:423
  12.1 0.8 %copy-start = (bf16[512,440]{1,0:T(8,128)(2,1)}, bf16[512,440]{1,0:T(8,128)(2,1)S(1)}, u32[]{:S(2)}) copy-start(bf16[512,440]{1,0:T(8,128)(2,1)S(1)} %get-tuple-element.20.vertical_ref) | copy-start | bytes 1351684
  19.8 4.8 %copy-start.1 = (bf16[512,440]{1,0:T(8,128)(2,1)S(1)}, bf16[512,440]{1,0:T(8,128)(2,1)}, u32[]{:S(2)}) copy-start(bf16[512,440]{1,0:T(8,128)(2,1)} %copy-done) | copy-start | bytes 1351684
  19.9 4.7 %collective-permute-start = (f32[192,128]{1,0:T(8,128)S(1)}, f32[192,128]{1,0:T(8,128)S(1)}, u32[]{:S(2)}, u32[]{:S(2)}) collective-permute-start(f32[192,128]{1,0:T(8,128)S(1)} %get-tuple-element.18), channel_id=1, source_target_pairs={{0,1},{2,3},{4,5},{6,7},{1,0},{3,2},{5,4},{7,6},{8,9},{10,11},{12,... | collective-permute-start | bytes 294920 | tf_op jit(solution)/shard_map/ppermute | solution.py:455
  21.0 3.6 %collective-permute-start.1 = (f32[192,128]{1,0:T(8,128)S(1)}, f32[192,128]{1,0:T(8,128)S(1)}, u32[]{:S(2)}, u32[]{:S(2)}) collective-permute-start(f32[192,128]{1,0:T(8,128)S(1)} %get-tuple-element.19), channel_id=1, source_target_pairs={{1,2},{3,4},{5,6},{2,1},{4,3},{6,5},{9,10},{11,12},{13,14},{10,9},... | collective-permute-start | bytes 294920 | tf_op jit(solution)/shard_map/ppermute | solution.py:455
  30.2 14.8 %all-to-all-start.1 = ((f32[8,64,128]{2,1,0:T(8,128)}), f32[8,64,128]{2,1,0:T(8,128)S(1)}, u32[]{:S(2)}, u32[]{:S(2)}) async-start(f32[8,64,128]{2,1,0:T(8,128)} %get-tuple-element.21), calls=%async_computation.1 | async-start | bytes 524288 | tf_op jit(solution)/shard_map/all_to_all | solution.py:491

commit v3 on v2

--- a/solution.py
+++ b/solution.py
@@ -12,6 +12,7 @@
 TW = 2304
 LANES = 128
 SLOTS = 32
+TAIL = 32
 
 gauss_sigmas = (0.7, 1.5, 3.0)
 poly_degrees = (4, 2, 2)
@@ -23,10 +24,12 @@
 basis_list = [
     (g, i, j) for g, top in enumerate(poly_degrees) for i in range(top + 1) for j in range(top + 1 - i)
 ]
-NB = len(basis_list)
 NF = len(filters)
-ONE = NB
-SCI = NB + 1
+HALF = SLOTS // 2
+filter_sets = [[f for f in filters if f[0] == 0], [f for f in filters if f[0] > 0]]
+image_sets = [[b for b in basis_list if b[0] == 0], [b for b in basis_list if b[0] > 0]]
+ONE = len(image_sets[0])
+SCI = HALF + len(image_sets[1])
 moment_keys = [(a, c) for c in range(5) for a in range(5 - c)]
 NQ = len(mono_powers)
 
@@ -87,52 +90,61 @@
     other_ref[count * H :, :] = jnp.zeros((spare, LANES), jnp.float32)
 
 
-def table_kernel(source_ref, owner_ref, horizontal_high_ref, horizontal_low_ref, vertical_ref, *, rows, halo):
+def table_kernel(source_ref, owner_ref, band_ref, *vertical_refs, rows, halo):
     me = lax.axis_index("ccd") * lax.axis_size("strip") + lax.axis_index("strip")
     source = source_ref[...]
     owner = jnp.sum(jnp.where(iota(source.shape, 1) == me, source, 0), axis=1, keepdims=True)
     owner_ref[...] = jnp.broadcast_to(owner, owner_ref.shape)
-    offset = (iota((2 * LANES, LANES), 0) - iota((2 * LANES, LANES), 1) - H).astype(jnp.float32)
-    inside = jnp.abs(offset) <= H
+    row = iota((LANES, LANES), 0)
+    near = row - iota((LANES, LANES), 1) - H
+    far = near + LANES - row + row % TAIL
     for f, (g, n) in enumerate(filters):
         sigma = gauss_sigmas[g]
-        tap = jnp.exp(-offset * offset / (2.0 * sigma * sigma)) * (1.0 / envelope_norm(sigma))
-        for _ in range(n):
-            tap = tap * (offset * (1.0 / sigma))
-        tap = jnp.where(inside, tap, 0.0)
-        tap_high, tap_low = split_two(tap)
-        horizontal_high_ref[:, f * LANES : (f + 1) * LANES] = tap_high
-        horizontal_low_ref[:, f * LANES : (f + 1) * LANES] = tap_low
-    width = vertical_ref.shape[1]
-    slot = iota((SLOTS, width), 0)
-    column = iota((SLOTS, width), 1)
-    wanted = jnp.full((SLOTS, width), -1, jnp.int32)
-    degree = jnp.zeros((SLOTS, width), jnp.int32)
-    scale = jnp.ones((SLOTS, width), jnp.float32)
-    weight = jnp.zeros((SLOTS, width), jnp.float32)
-    for b, (g, i, j) in enumerate(basis_list):
-        here = slot == b
-        wanted = jnp.where(here, filters.index((g, i)), wanted)
-        degree = jnp.where(here, j, degree)
-        scale = jnp.where(here, 1.0 / gauss_sigmas[g], scale)
-        weight = jnp.where(here, 1.0 / envelope_norm(gauss_sigmas[g]), weight)
-    own = column - wanted * rows
-    outside = column - NF * rows - wanted * halo
-    is_own = (own >= 0) & (own < rows)
-    is_above = (outside >= 0) & (outside < H)
-    is_below = (outside >= H) & (outside < 2 * H)
-    is_own = is_own & (column < NF * rows)
-    row_in = jnp.where(is_own, own + H, jnp.where(is_below, outside + rows, outside))
-    matched = is_own | ((column >= NF * rows) & (is_above | is_below))
-    for r in range(rows):
-        a = row_in - (r + H)
-        z = a.astype(jnp.float32) * scale
-        tap = jnp.exp(-0.5 * z * z) * weight
-        square = z * z
-        power = jnp.where(degree == 1, z, jnp.where(degree == 2, square, 1.0))
-        power = jnp.where(degree == 3, square * z, jnp.where(degree == 4, square * square, power))
-        keep = matched & (jnp.abs(a) <= H)
-        vertical_ref[r * SLOTS : (r + 1) * SLOTS, :] = jnp.where(keep, tap * power, 0.0).astype(jnp.bfloat16)
+        at = slice(f * LANES, (f + 1) * LANES)
+        parts = []
+        for place in (near, far):
+            offset = place.astype(jnp.float32)
+            tap = jnp.exp(-offset * offset / (2.0 * sigma * sigma)) * (1.0 / envelope_norm(sigma))
+            for _ in range(n):
+                tap = tap * (offset * (1.0 / sigma))
+            parts.append(split_two(jnp.where(jnp.abs(place) <= H, tap, 0.0)))
+        (near_high, near_low), (far_high, far_low) = parts
+        band_ref[0:LANES, at] = near_high
+        band_ref[LANES : 2 * LANES, at] = near_high
+        band_ref[2 * LANES : 3 * LANES, at] = near_low
+        tail = jnp.where(row < 2 * TAIL, far_high.astype(jnp.float32), far_low.astype(jnp.float32))
+        band_ref[3 * LANES :, at] = jnp.where(row < 3 * TAIL, tail, 0.0).astype(jnp.bfloat16)
+    for vertical_ref, members, images in zip(vertical_refs, filter_sets, image_sets):
+        width = vertical_ref.shape[1]
+        slot = iota((HALF, width), 0)
+        column = iota((HALF, width), 1)
+        wanted = jnp.full((HALF, width), -1, jnp.int32)
+        degree = jnp.zeros((HALF, width), jnp.int32)
+        scale = jnp.ones((HALF, width), jnp.float32)
+        weight = jnp.zeros((HALF, width), jnp.float32)
+        for b, (g, i, j) in enumerate(images):
+            here = slot == b
+            wanted = jnp.where(here, members.index((g, i)), wanted)
+            degree = jnp.where(here, j, degree)
+            scale = jnp.where(here, 1.0 / gauss_sigmas[g], scale)
+            weight = jnp.where(here, 1.0 / envelope_norm(gauss_sigmas[g]), weight)
+        edge = len(members) * rows
+        own = column - wanted * rows
+        outside = column - edge - wanted * halo
+        is_own = (own >= 0) & (own < rows) & (column < edge)
+        is_above = (outside >= 0) & (outside < H)
+        is_below = (outside >= H) & (outside < 2 * H)
+        row_in = jnp.where(is_own, own + H, jnp.where(is_below, outside + rows, outside))
+        matched = (is_own | ((column >= edge) & (is_above | is_below))) & (wanted >= 0)
+        for r in range(rows):
+            a = row_in - (r + H)
+            z = a.astype(jnp.float32) * scale
+            tap = jnp.exp(-0.5 * z * z) * weight
+            square = z * z
+            power = jnp.where(degree == 1, z, jnp.where(degree == 2, square, 1.0))
+            power = jnp.where(degree == 3, square * z, jnp.where(degree == 4, square * square, power))
+            keep = matched & (jnp.abs(a) <= H)
+            vertical_ref[r * HALF : (r + 1) * HALF, :] = jnp.where(keep, tap * power, 0.0).astype(jnp.bfloat16)
 
 
 def wide_tile(value):
@@ -149,32 +161,45 @@
     return 2.0 * (iota((1, cols), 1).astype(jnp.float32) + 0.5) / cols - 1.0
 
 
-def filter_rows(padded, high_ref, low_ref, filtered_ref, out_ref):
+def filter_rows(padded, band_ref, filtered_ref, out_refs):
     count = padded.shape[0]
     blocks = filtered_ref.shape[0] // count
-    window = [split_two(padded[:, w * LANES : (w + 1) * LANES]) for w in range(blocks + 1)]
+    lane = iota((count, LANES), 1)
+    window, tails = [], []
+    for w in range(blocks + 1):
+        tile = padded[:, w * LANES : (w + 1) * LANES]
+        high, low = split_two(tile)
+        window.append((high, low))
+        high, low = high.astype(jnp.float32), low.astype(jnp.float32)
+        tail = jnp.where(lane < 2 * TAIL, pltpu.roll(low, TAIL, 1), pltpu.roll(high, 2 * TAIL, 1))
+        tails.append(jnp.where(lane < TAIL, high, tail).astype(jnp.bfloat16))
     left = []
     for w in range(blocks):
-        (h0, l0), (h1, l1) = window[w], window[w + 1]
-        left.append(jnp.concatenate([h0, h1, l0, l1, h0, h1], axis=1))
-    left = jnp.concatenate(left, axis=0)
-    right = jnp.concatenate([high_ref[...], high_ref[...], low_ref[...]], axis=0)
-    filtered_ref[...] = jnp.dot(left, right, preferred_element_type=jnp.float32)
+        high, low = window[w]
+        left.append(jnp.concatenate([high, low, high, tails[w + 1]], axis=1))
+    filtered_ref[...] = jnp.dot(
+        jnp.concatenate(left, axis=0), band_ref[...], preferred_element_type=jnp.float32
+    )
     for w in range(blocks):
-        out_ref[:, w * LANES : (w + 1) * LANES] = jnp.concatenate(
-            [filtered_ref[w * count : (w + 1) * count, f * LANES : (f + 1) * LANES] for f in range(NF)],
-            axis=0,
-        ).astype(jnp.bfloat16)
-
-
-def own_kernel(window_ref, high_ref, low_ref, out_ref, filtered_ref):
-    filter_rows(window_ref[...], high_ref, low_ref, filtered_ref, out_ref)
+        for out_ref, members in zip(out_refs, filter_sets):
+            first = filters.index(members[0])
+            out_ref[:, w * LANES : (w + 1) * LANES] = jnp.concatenate(
+                [
+                    filtered_ref[w * count : (w + 1) * count, f * LANES : (f + 1) * LANES]
+                    for f in range(first, first + len(members))
+                ],
+                axis=0,
+            ).astype(jnp.bfloat16)
+
+
+def own_kernel(window_ref, band_ref, *refs):
+    filter_rows(window_ref[...], band_ref, refs[-1], refs[:-1])
 
 
 def basis_kernel(
-    own_ref, partner_ref, other_ref, science_hbm_ref, high_ref, low_ref, vertical_ref,
-    basis_ref, moment_out_ref,
-    padded_ref, filtered_ref, outside_ref, science_ref, moment_ref, sems,
+    first_own_ref, second_own_ref, partner_ref, other_ref, science_hbm_ref, band_ref, first_ref, second_ref,
+    basis_ref, moment_ref,
+    padded_ref, filtered_ref, first_outside_ref, second_outside_ref, science_ref, sems,
 ):
     strip_count = lax.axis_size("strip")
     strip = lax.axis_index("strip")
@@ -189,22 +214,28 @@
         partner, other = partner_ref[w * H : (w + 1) * H, :], other_ref[w * H : (w + 1) * H, :]
         padded_ref[0:H, at] = jnp.where(even, other, partner)
         padded_ref[H : 2 * H, at] = jnp.where(even, partner, other)
-    filter_rows(padded_ref[...], high_ref, low_ref, filtered_ref, outside_ref)
+    filter_rows(padded_ref[...], band_ref, filtered_ref, (first_outside_ref, second_outside_ref))
 
     eighth = iota((8, 2 * LANES), 0)
     science_copy.wait()
     for pair in range(blocks // 2):
         at = slice(pair * 2 * LANES, (pair + 1) * 2 * LANES)
-        block = jnp.dot(
-            vertical_ref[...],
-            jnp.concatenate([own_ref[:, at], outside_ref[:, at]], axis=0),
-            preferred_element_type=jnp.float32,
+        one, two = (
+            jnp.dot(
+                vertical_ref[...],
+                jnp.concatenate([own_ref[:, at], outside_ref[:, at]], axis=0),
+                preferred_element_type=jnp.float32,
+            )
+            for vertical_ref, own_ref, outside_ref in (
+                (first_ref, first_own_ref, first_outside_ref),
+                (second_ref, second_own_ref, second_outside_ref),
+            )
         )
         parts = []
         for r in range(rows):
-            last = block[(r + 1) * SLOTS - 8 : (r + 1) * SLOTS]
-            last = jnp.where(eighth == ONE % 8, 1.0, jnp.where(eighth == SCI % 8, science_ref[r : r + 1, at], last))
-            parts += [block[r * SLOTS : (r + 1) * SLOTS - 8], last]
+            low, high = r * HALF, (r + 1) * HALF
+            parts += [one[low : high - 8], jnp.where(eighth == ONE % 8, 1.0, one[high - 8 : high])]
+            parts += [two[low : high - 8], jnp.where(eighth == SCI % 8, science_ref[r : r + 1, at], two[high - 8 : high])]
         basis_ref[:, at] = jnp.concatenate(parts, axis=0).astype(jnp.bfloat16)
     u = u_row(cols)
     square = u * u
@@ -212,11 +243,12 @@
     for r in range(rows):
         here = basis_ref[r * SLOTS : (r + 1) * SLOTS, :]
         wide = here.astype(jnp.float32)
-        design = jnp.concatenate(
-            [here, (wide * u).astype(jnp.bfloat16), (wide * square).astype(jnp.bfloat16)], axis=0
-        )
+        once, twice = (wide * u).astype(jnp.bfloat16), (wide * square).astype(jnp.bfloat16)
         product = lax.dot_general(
-            design, design, (((1,), (1,)), ((), ())), preferred_element_type=jnp.float32
+            jnp.concatenate([here, once, twice], axis=0),
+            jnp.concatenate([here, twice], axis=0),
+            (((1,), (1,)), ((), ())),
+            preferred_element_type=jnp.float32,
         )
         v = 2.0 * ((strip * rows + r).astype(jnp.float32) + 0.5) / (rows * strip_count) - 1.0
         for c in range(5):
@@ -227,7 +259,7 @@
     lane = iota((half, LANES), 1)
     chunks = [jnp.zeros((half, LANES), jnp.float32) for _ in range(moment_ref.shape[0] // half)]
     for at, (a, c) in enumerate(moment_keys):
-        first, second = (a, 0) if a < 3 else (a - 2, 2)
+        first, second = (a, 0) if a < 3 else (a - 2, 1)
         group = at % 4 * SLOTS
         top = totals[c][first * SLOTS : first * SLOTS + half, :]
         bottom = totals[c][first * SLOTS + half : (first + 1) * SLOTS, :]
@@ -237,27 +269,19 @@
         chunks[at // 4] = jnp.where(lane // SLOTS == at % 4, both, chunks[at // 4])
     for p, chunk in enumerate(chunks):
         moment_ref[p * half : (p + 1) * half, :] = chunk
-    sends = []
-    for k in range(moment_out_ref.shape[0]):
-        sends.append(pltpu.make_async_copy(moment_ref, moment_out_ref.at[k], sems.at[1 + k]))
-        sends[k].start()
-    for send in sends:
-        send.wait()
-
-
-def solve_kernel(
-    moment_ref, order_ref, science_hbm_ref, basis_ref, out_ref,
-    system_ref, science_ref, sem,
-):
+
+
+def solve_kernel(order_ref, science_hbm_ref, basis_ref, *refs):
+    out_hbm_ref, system_ref, science_ref, out_ref, sem, sems = refs[-6:]
     strip_count = lax.axis_size("strip")
     strip = lax.axis_index("strip")
     rows, cols = science_ref.shape
     copy = pltpu.make_async_copy(science_hbm_ref, science_ref, sem)
     copy.start()
     order = order_ref[0]
-    total = moment_ref[0]
-    for k in range(1, moment_ref.shape[0]):
-        total = total + moment_ref[k]
+    total = refs[0][...]
+    for ref in refs[1:-6]:
+        total = total + ref[...]
     half = SLOTS // 2
     across = jnp.transpose(jnp.concatenate([total, jnp.zeros((LANES - total.shape[0], LANES), jnp.float32)], axis=0))
     next_across = pltpu.roll(across, LANES - 1, 0)
@@ -285,7 +309,7 @@
     row_slot = iota((SLOTS, LANES), 0)
 
     def active(slot, q):
-        return ((slot < NB) & (mono_degrees[q] <= order)) | (slot == ONE)
+        return ((slot < SCI) & (slot != ONE) & (mono_degrees[q] <= order)) | (slot == ONE)
 
     def moved(key, to_lane, from_lane):
         return turn_lanes(pieces[key], to_lane - from_lane)
@@ -314,6 +338,11 @@
     def column(value, at):
         return jnp.broadcast_to(value[:, at : at + 1], (8, LANES))
 
+    def added(terms):
+        while len(terms) > 1:
+            terms = [sum(terms[n + 1 : n + 2], terms[n]) for n in range(0, len(terms), 2)]
+        return terms[0]
+
     def row_of(value, at):
         return jnp.broadcast_to(value[at : at + 1, :], (8, LANES))
 
@@ -323,14 +352,21 @@
         inner = list(range(q * per, (q + 1) * per))
         for block in inner:
             first = 8 * block % LANES
-            count = min(8, NB + 1 - 8 * block % SLOTS)
+            count = min(8, SCI - 8 * block % SLOTS)
             panel = [column(groups[block][side], first + j) for j in range(count)] + groups[block][side:]
-            for k in range(count):
-                inverse = 1.0 / row_of(panel[k], k)
-                pivot = row8 == k
-                factor = jnp.where(pivot, inverse, -panel[k] * inverse)
-                for j in range(k + 1, len(panel)):
-                    panel[j] = jnp.where(pivot, 0.0, panel[j]) + factor * row_of(panel[j], k)
+            for k in range(0, count, 2):
+                one, two = panel[k], panel[k + 1]
+                a, b = row_of(one, k), row_of(two, k)
+                c, d = row_of(one, k + 1), row_of(two, k + 1)
+                inverse = 1.0 / (a * d - b * c)
+                here, after = row8 == k, row8 == k + 1
+                first_factor = inverse * jnp.where(here, d, jnp.where(after, -c, two * c - one * d))
+                second_factor = inverse * jnp.where(here, -b, jnp.where(after, a, one * b - two * a))
+                for j in range(k + 2, len(panel)):
+                    old = jnp.where(here | after, 0.0, panel[j])
+                    panel[j] = old + (
+                        first_factor * row_of(panel[j], k) + second_factor * row_of(panel[j], k + 1)
+                    )
             ready = panel[count:]
             spread_rows = [[row_of(tile, j) for j in range(count)] for tile in ready]
             groups[block][side:] = ready
@@ -338,14 +374,14 @@
                 if i != block:
                     factors = [column(groups[i][side], first + j) for j in range(count)]
                     for t in range(side, 2):
-                        for j in range(count):
-                            groups[i][t] = groups[i][t] - factors[j] * spread_rows[t - side][j]
+                        products = [factors[j] * spread_rows[t - side][j] for j in range(count)]
+                        groups[i][t] = groups[i][t] - added(products)
         ahead = list(range((q + 1) * per, (q + 2) * per)) if q + 1 < NQ else []
         for i in ahead:
-            factors = [column(groups[i][side], start + j) for j in range(NB + 1)]
+            factors = [column(groups[i][side], start + j) for j in range(SCI)]
             for t in range(side, 2):
-                for j in range(NB + 1):
-                    groups[i][t] = groups[i][t] - factors[j] * row_of(groups[inner[j // 8]][t], j % 8)
+                products = [factors[j] * row_of(groups[inner[j // 8]][t], j % 8) for j in range(SCI)]
+                groups[i][t] = groups[i][t] - added(products)
         rest = [i for i in range(len(groups)) if i not in inner and i not in ahead]
         left = jnp.concatenate([groups[i][side] for i in rest], axis=0)
         right = jnp.concatenate([jnp.concatenate([groups[i][t] for i in inner], axis=0) for t in range(side, 2)], axis=1)
@@ -380,10 +416,18 @@
     spread_high, spread_low = split_two(spread)
     spread = jnp.concatenate([spread_high, spread_low], axis=0)
     copy.wait()
-    sums = jnp.dot(spread, basis_ref[...], preferred_element_type=jnp.float32)
     u = u_row(cols)
-    model = [sums[a * rows : (a + 1) * rows] + sums[(a + 3) * rows : (a + 4) * rows] for a in range(3)]
-    out_ref[...] = science_ref[...] - (model[0] + u * (model[1] + u * model[2]))
+    step = cols // sems.shape[0]
+    writes = []
+    for n in range(sems.shape[0]):
+        at = slice(n * step, (n + 1) * step)
+        sums = jnp.dot(spread, basis_ref[:, at], preferred_element_type=jnp.float32)
+        model = [sums[a * rows : (a + 1) * rows] + sums[(a + 3) * rows : (a + 4) * rows] for a in range(3)]
+        out_ref[:, at] = science_ref[:, at] - (model[0] + u[:, at] * (model[1] + u[:, at] * model[2]))
+        writes.append(pltpu.make_async_copy(out_ref.at[:, at], out_hbm_ref.at[:, at], sems.at[n]))
+        writes[n].start()
+    for write in writes:
+        write.wait()
 
 
 def body(tile_store, tile_source, tile_slot, shift_cols, spatial_order, science):
@@ -421,16 +465,15 @@
         name="pack",
     )(tile_store, source, slot)
     arrived = lax.all_to_all(outgoing, ("ccd", "strip"), split_axis=0, concat_axis=0, tiled=True)
-    owner, taps_high, taps_low, vertical = pl.pallas_call(
+    owner, band, *vertical = pl.pallas_call(
         lambda *refs: table_kernel(*refs, rows=rows, halo=halo),
         out_shape=(
             pltpu.VMEM((tile_source.shape[1], LANES), jnp.int32),
-            pltpu.VMEM((2 * LANES, NF * LANES), jnp.bfloat16),
-            pltpu.VMEM((2 * LANES, NF * LANES), jnp.bfloat16),
-            pltpu.VMEM((rows * SLOTS, NF * (rows + halo)), jnp.bfloat16),
-        ),
+            pltpu.VMEM((4 * LANES, NF * LANES), jnp.bfloat16),
+        )
+        + tuple(pltpu.VMEM((rows * HALF, len(m) * (rows + halo)), jnp.bfloat16) for m in filter_sets),
         in_specs=[vmem],
-        out_specs=(vmem, vmem, vmem, vmem),
+        out_specs=(vmem,) * 4,
         compiler_params=params(16),
         name="tables",
         cost_estimate=pl.CostEstimate(flops=10_000_000, bytes_accessed=2_000_000, transcendentals=1_000_000),
@@ -459,50 +502,57 @@
 
     filtered_own = pl.pallas_call(
         own_kernel,
-        out_shape=pltpu.VMEM((NF * rows, cols), jnp.bfloat16),
-        in_specs=[vmem, vmem, vmem],
-        out_specs=vmem,
+        out_shape=tuple(pltpu.VMEM((len(m) * rows, cols), jnp.bfloat16) for m in filter_sets),
+        in_specs=[vmem, vmem],
+        out_specs=(vmem, vmem),
         scratch_shapes=[pltpu.VMEM((cols // LANES * rows, NF * LANES), jnp.float32)],
         compiler_params=params(16),
         name="own",
         cost_estimate=pl.CostEstimate(flops=600_000_000, bytes_accessed=3_000_000, transcendentals=0),
-    )(window, kept(taps_high), kept(taps_low))
+    )(window, kept(band))
     half = SLOTS // 2
     packed = -(-len(moment_keys) // 4) * half
     basis, moments = pl.pallas_call(
         basis_kernel,
         out_shape=(
             pltpu.VMEM((rows * SLOTS, cols), jnp.bfloat16),
-            pltpu.HBM((strip_count, packed, LANES), jnp.float32),
+            pltpu.VMEM((packed, LANES), jnp.float32),
         ),
-        in_specs=[vmem, vmem, vmem, hbm, vmem, vmem, vmem],
-        out_specs=(vmem, hbm),
+        in_specs=[vmem, vmem, vmem, vmem, hbm, vmem, vmem, vmem],
+        out_specs=(vmem, vmem),
         scratch_shapes=[
             pltpu.VMEM((halo, count * LANES), jnp.float32),
             pltpu.VMEM((cols // LANES * halo, NF * LANES), jnp.float32),
-            pltpu.VMEM((NF * halo, cols), jnp.bfloat16),
+            pltpu.VMEM((len(filter_sets[0]) * halo, cols), jnp.bfloat16),
+            pltpu.VMEM((len(filter_sets[1]) * halo, cols), jnp.bfloat16),
             pltpu.VMEM((rows, cols), jnp.float32),
-            pltpu.VMEM((packed, LANES), jnp.float32),
-            pltpu.SemaphoreType.DMA((1 + strip_count,)),
+            pltpu.SemaphoreType.DMA((1,)),
         ],
         compiler_params=params(24),
         name="basis",
-    )(kept(filtered_own), from_partner, from_other, science, kept(taps_high), kept(taps_low), kept(vertical))
-    gathered = lax.all_to_all(moments, "strip", split_axis=0, concat_axis=0, tiled=True)
+    )(*map(kept, filtered_own), from_partner, from_other, science, *map(kept, (band, *vertical)))
+
+    def exchanged(value, step):
+        return lax.ppermute(value, "strip", [(i, i ^ step) for i in range(strip_count)])
+
+    moments = moments + exchanged(moments, 1)
+    parts = [moments] + [exchanged(moments, step) for step in range(2, strip_count, 2)]
 
     return pl.pallas_call(
         solve_kernel,
         out_shape=jax.ShapeDtypeStruct((rows, cols), jnp.float32),
-        in_specs=[vmem, smem, hbm, vmem],
-        out_specs=vmem,
+        in_specs=[smem, hbm, vmem] + [vmem] * len(parts),
+        out_specs=hbm,
         scratch_shapes=[
             pltpu.VMEM((NQ * SLOTS, 2 * LANES), jnp.float32),
             pltpu.VMEM((rows, cols), jnp.float32),
+            pltpu.VMEM((rows, cols), jnp.float32),
             pltpu.SemaphoreType.DMA,
+            pltpu.SemaphoreType.DMA((4,)),
         ],
         compiler_params=params(16),
         name="solve",
-    )(gathered, spatial_order, science, kept(basis))
+    )(spatial_order, science, kept(basis), *parts)
 
 
 def solution(mesh):

time: 53.8 us -> 51.6 us (0.959)
  Pallas kernels: 19 us -> 15.3 us
  starting transfers between devices: 15.6 us -> 18.3 us
  local copies, waits for them, and re-layouts: 0.79 us -> 0 us
    ppermute x0 -> x4, starting transfers between devices: none -> 9.24 us  [exchanged(): lax.ppermute(value, 'strip', [(i, i ^ step) for i in range(strip_count)])]
    all_to_all x1 -> x0, waiting for transfers between devices: 7.57 us -> none  [body(): lax.all_to_all(moments, 'strip', split_axis=0, concat_axis=0, tiled=True)]
    all_to_all x1 -> x0, starting transfers between devices: 6.53 us -> none  [body(): lax.all_to_all(moments, 'strip', split_axis=0, concat_axis=0, tiled=True)]
    ppermute x0 -> x4, waiting for transfers between devices: none -> 5.58 us  [exchanged(): lax.ppermute(value, 'strip', [(i, i ^ step) for i in range(strip_count)])]
    pallas_call x1, Pallas kernels: 5.55 us -> 3.96 us  [body(): pl.pallas_call(basis_kernel, out_shape=(pltpu.VMEM((rows * SLOTS, cols),...]
    all_to_all x1, waiting for transfers between devices: 6.87 us -> 8.4 us  [body(): lax.all_to_all(outgoing, ('ccd', 'strip'), split_axis=0, concat_axis=0, t...]
    pallas_call x1, Pallas kernels: 8.42 us -> 7.15 us  [body(): pl.pallas_call(solve_kernel, out_shape=jax.ShapeDtypeStruct((rows, cols),...]
    unnamed x4 -> x0, local copies, waits for them, and re-layouts: 0.79 us -> none
  transfers between devices with their start and end apart: 4 -> 7, of which waited for: 3 -> 5; matrix products, arithmetic and copies ran while one was open for 0% -> 0% of each run, Pallas kernels for 6% -> 4%
where the time goes in v3:
time: 51.6 us; the launch traced here: 51.2 us
  starting transfers between devices  18.3 us (35%)
  waiting for transfers between devices  16.3 us (32%)
  Pallas kernels  15.3 us (30%)
  between operations  1.36 us (3%)
    ppermute x4, starting transfers between devices, exchanged(): lax.ppermute(value, 'strip', [(i, i ^ step) for i in range(strip_count)])  9.24 us
    all_to_all x1, waiting for transfers between devices, body(): lax.all_to_all(outgoing, ('ccd', 'strip'), split_axis=0, concat_axis=0, t...  8.4 us
    all_to_all x1, starting transfers between devices, body(): lax.all_to_all(outgoing, ('ccd', 'strip'), split_axis=0, concat_axis=0, t...  7.3 us
    pallas_call x1, Pallas kernels, body(): pl.pallas_call(solve_kernel, out_shape=jax.ShapeDtypeStruct((rows, cols),...  7.15 us
    ppermute x4, waiting for transfers between devices, exchanged(): lax.ppermute(value, 'strip', [(i, i ^ step) for i in range(strip_count)])  5.58 us
    pallas_call x1, Pallas kernels, body(): pl.pallas_call(basis_kernel, out_shape=(pltpu.VMEM((rows * SLOTS, cols),...  3.96 us
    ppermute x2, waiting for transfers between devices, swap(): return lax.ppermute(value, 'strip', pairs + [(j, i) for i, j in pairs])  2.33 us
    pallas_call x1, Pallas kernels, body(): pl.pallas_call(pack_kernel, out_shape=jax.ShapeDtypeStruct((device_count,...  1.81 us
  transfers between devices with their start and end apart: 7, of which 5 were waited for; matrix products, arithmetic and copies ran while one was open for 0% of the time, Pallas kernels for 4%

profile of v3, /device:TPU:0, one launch (start us, length us, event | category | flops | bytes accessed | tf_op | source)
XLA Modules:
  0.0 51.2 jit_solution(12148941928142120580)
XLA Ops:
  0.0 1.8 %pack.1 = f32[32,16,128]{2,1,0:T(8,128)} custom-call(f32[18,16,128]{2,1,0:T(8,128)} %store_hbm_ref.1, s32[18,32]{1,0:T(8,128)} %bitcast.3, s32[18,32]{1,0:T(8,128)} %bitcast.2), custom_call_target="tpu_custom_call" | custom-call | tf_op jit(solution)/shard_map/pack/pallas_call | solution.py:453
  1.8 7.3 %all-to-all-start = ((f32[32,16,128]{2,1,0:T(8,128)}), f32[32,16,128]{2,1,0:T(8,128)S(1)}, u32[]{:S(2)}, u32[]{:S(2)}) async-start(f32[32,16,128]{2,1,0:T(8,128)} %pack.1), calls=%async_computation | async-start | bytes 524288 | tf_op jit(solution)/shard_map/all_to_all | solution.py:467
  9.8 1.6 %tables.1 = (s32[18,128]{1,0:T(8,128)S(1)}, bf16[512,1408]{1,0:T(8,128)(2,1)S(1)}, bf16[256,200]{1,0:T(8,128)(2,1)S(1)}, bf16[256,240]{1,0:T(8,128)(2,1)S(1)}) custom-call(s32[18,32]{1,0:T(8,128)} %bitcast.4), custom_call_target="tpu_custom_call" | custom-call | flops 10000000 | bytes 2000000 | tf_op jit(solution)/shard_map/tables/pallas_call | solution.py:468
  11.4 8.4 %all-to-all-done.arrived_ref = f32[32,16,128]{2,1,0:T(8,128)S(1)} async-done(((f32[32,16,128]{2,1,0:T(8,128)}), f32[32,16,128]{2,1,0:T(8,128)S(1)}, u32[]{:S(2)}, u32[]{:S(2)}) %all-to-all-start) | async-done | bytes 262176 | tf_op jit(solution)/shard_map/all_to_all | solution.py:467
  19.8 0.1 window.1
  19.9 1.1 %collective-permute-start = (f32[192,128]{1,0:T(8,128)S(1)}, f32[192,128]{1,0:T(8,128)S(1)}, u32[]{:S(2)}, u32[]{:S(2)}) collective-permute-start(f32[192,128]{1,0:T(8,128)S(1)} %get-tuple-element.21), channel_id=1, source_target_pairs={{0,1},{2,3},{4,5},{6,7},{1,0},{3,2},{5,4},{7,6},{8,9},{10,11},{12,... | collective-permute-start | bytes 294920 | tf_op jit(solution)/shard_map/ppermute | solution.py:498
  21.0 0.7 %collective-permute-start.1 = (f32[192,128]{1,0:T(8,128)S(1)}, f32[192,128]{1,0:T(8,128)S(1)}, u32[]{:S(2)}, u32[]{:S(2)}) collective-permute-start(f32[192,128]{1,0:T(8,128)S(1)} %get-tuple-element.22), channel_id=1, source_target_pairs={{1,2},{3,4},{5,6},{2,1},{4,3},{6,5},{9,10},{11,12},{13,14},{10,9},... | collective-permute-start | bytes 294920 | tf_op jit(solution)/shard_map/ppermute | solution.py:498
  21.7 0.6 %own.1 = (bf16[80,2048]{1,0:T(8,128)(2,1)S(1)}, bf16[96,2048]{1,0:T(8,128)(2,1)S(1)}) custom-call(f32[16,2176]{1,0:T(8,128)S(1)} %get-tuple-element.17.window_ref, bf16[512,1408]{1,0:T(8,128)(2,1)S(1)} %get-tuple-element.18.band_ref), custom_call_target="tpu_custom_call" | custom-call | flops 600000000 | bytes 3000000 | tf_op jit(solution)/shard_map/own/pallas_call | solution.py:503
  22.3 2.3 %collective-permute-done.partner_ref = f32[192,128]{1,0:T(8,128)S(1)} collective-permute-done((f32[192,128]{1,0:T(8,128)S(1)}, f32[192,128]{1,0:T(8,128)S(1)}, u32[]{:S(2)}, u32[]{:S(2)}) %collective-permute-start) | collective-permute-done | bytes 98336 | tf_op jit(solution)/shard_map/ppermute | solution.py:498
  24.6 0.0 collective-permute-done.1.other_ref
  24.6 4.0 %basis.1 = (bf16[512,2048]{1,0:T(8,128)(2,1)S(1)}, f32[64,128]{1,0:T(8,128)S(1)}) custom-call(bf16[80,2048]{1,0:T(8,128)(2,1)S(1)} %get-tuple-element.19.first_own_ref, bf16[96,2048]{1,0:T(8,128)(2,1)S(1)} %get-tuple-element.20.second_own_ref, f32[192,128]{1,0:T(8,128)S(1)} %collective-permute-done.partner_ref, ...), custom_call_target="tpu_custom_call" | custom-call | tf_op jit(solution)/shard_map/basis/pallas_call | solution.py:515
  28.6 4.9 %collective-permute-start.2 = (f32[64,128]{1,0:T(8,128)S(1)}, f32[64,128]{1,0:T(8,128)S(1)}, u32[]{:S(2)}, u32[]{:S(2)}) collective-permute-start(f32[64,128]{1,0:T(8,128)S(1)} %get-tuple-element.26), channel_id=1, source_target_pairs={{0,1},{1,0},{2,3},{3,2},{4,5},{5,4},{6,7},{7,6},{8,9},{9,8},{10,11... | collective-permute-start | bytes 98312 | tf_op jit(solution)/shard_map/ppermute | solution.py:536
  33.4 1.9 %collective-permute-done.2 = f32[64,128]{1,0:T(8,128)S(1)} collective-permute-done((f32[64,128]{1,0:T(8,128)S(1)}, f32[64,128]{1,0:T(8,128)S(1)}, u32[]{:S(2)}, u32[]{:S(2)}) %collective-permute-start.2) | collective-permute-done | bytes 32800 | tf_op jit(solution)/shard_map/ppermute | solution.py:536
  35.3 1.2 %collective-permute-start.3 = (f32[64,128]{1,0:T(8,128)S(1)}, f32[64,128]{1,0:T(8,128)S(1)}, u32[]{:S(2)}, u32[]{:S(2)}) collective-permute-start(f32[64,128]{1,0:T(8,128)S(1)} %add.3.refs_0_), channel_id=1, source_target_pairs={{0,2},{1,3},{2,0},{3,1},{4,6},{5,7},{6,4},{7,5},{8,10},{9,11},{10,... | collective-permute-start | bytes 98312 | tf_op jit(solution)/shard_map/ppermute | solution.py:536
  36.5 1.9 %collective-permute-start.4 = (f32[64,128]{1,0:T(8,128)S(1)}, f32[64,128]{1,0:T(8,128)S(1)}, u32[]{:S(2)}, u32[]{:S(2)}) collective-permute-start(f32[64,128]{1,0:T(8,128)S(1)} %add.3.refs_0_), channel_id=1, source_target_pairs={{0,4},{1,5},{2,6},{3,7},{4,0},{5,1},{6,2},{7,3},{8,12},{9,13},{10,... | collective-permute-start | bytes 98312 | tf_op jit(solution)/shard_map/ppermute | solution.py:536
  38.4 1.4 %collective-permute-start.5 = (f32[64,128]{1,0:T(8,128)S(1)}, f32[64,128]{1,0:T(8,128)S(1)}, u32[]{:S(2)}, u32[]{:S(2)}) collective-permute-start(f32[64,128]{1,0:T(8,128)S(1)} %add.3.refs_0_), channel_id=1, source_target_pairs={{0,6},{1,7},{2,4},{3,5},{4,2},{5,3},{6,0},{7,1},{8,14},{9,15},{10,... | collective-permute-start | bytes 98312 | tf_op jit(solution)/shard_map/ppermute | solution.py:536
  40.4 0.0 collective-permute-done.3.refs_1_
  40.4 0.9 %collective-permute-done.4.refs_2_ = f32[64,128]{1,0:T(8,128)S(1)} collective-permute-done((f32[64,128]{1,0:T(8,128)S(1)}, f32[64,128]{1,0:T(8,128)S(1)}, u32[]{:S(2)}, u32[]{:S(2)}) %collective-permute-start.4) | collective-permute-done | bytes 32800 | tf_op jit(solution)/shard_map/ppermute | solution.py:536
  41.3 2.7 %collective-permute-done.5.refs_3_ = f32[64,128]{1,0:T(8,128)S(1)} collective-permute-done((f32[64,128]{1,0:T(8,128)S(1)}, f32[64,128]{1,0:T(8,128)S(1)}, u32[]{:S(2)}, u32[]{:S(2)}) %collective-permute-start.5) | collective-permute-done | bytes 32800 | tf_op jit(solution)/shard_map/ppermute | solution.py:536
  44.1 7.2 %solve.1 = f32[16,2048]{1,0:T(8,128)} custom-call(s32[1]{0:T(128)S(6)} %copy.8.order_ref, f32[16,2048]{1,0:T(8,128)} %science_hbm_ref.3, bf16[512,2048]{1,0:T(8,128)(2,1)S(1)} %get-tuple-element.25.basis_ref, f32[64,128]{1,0:T(8,128)S(1)} %add.3.refs_0_, f32[64,128]{1,0:T(8,128)S(1)} %collective-permute-done.3.refs_1_, ...), custom_call_target="tpu_custom_call" | custom-call | tf_op jit(solution)/shard_map/solve/pallas_call | solution.py:541
  (1 shorter events, 0.0 us)
Async XLA Ops:
  1.8 18.0 %all-to-all-start = ((f32[32,16,128]{2,1,0:T(8,128)}), f32[32,16,128]{2,1,0:T(8,128)S(1)}, u32[]{:S(2)}, u32[]{:S(2)}) async-start(f32[32,16,128]{2,1,0:T(8,128)} %pack.1), calls=%async_computation | async-start | bytes 524288 | tf_op jit(solution)/shard_map/all_to_all | solution.py:467
  19.9 4.7 %collective-permute-start = (f32[192,128]{1,0:T(8,128)S(1)}, f32[192,128]{1,0:T(8,128)S(1)}, u32[]{:S(2)}, u32[]{:S(2)}) collective-permute-start(f32[192,128]{1,0:T(8,128)S(1)} %get-tuple-element.21), channel_id=1, source_target_pairs={{0,1},{2,3},{4,5},{6,7},{1,0},{3,2},{5,4},{7,6},{8,9},{10,11},{12,... | collective-permute-start | bytes 294920 | tf_op jit(solution)/shard_map/ppermute | solution.py:498
  21.0 3.6 %collective-permute-start.1 = (f32[192,128]{1,0:T(8,128)S(1)}, f32[192,128]{1,0:T(8,128)S(1)}, u32[]{:S(2)}, u32[]{:S(2)}) collective-permute-start(f32[192,128]{1,0:T(8,128)S(1)} %get-tuple-element.22), channel_id=1, source_target_pairs={{1,2},{3,4},{5,6},{2,1},{4,3},{6,5},{9,10},{11,12},{13,14},{10,9},... | collective-permute-start | bytes 294920 | tf_op jit(solution)/shard_map/ppermute | solution.py:498
  28.6 6.8 %collective-permute-start.2 = (f32[64,128]{1,0:T(8,128)S(1)}, f32[64,128]{1,0:T(8,128)S(1)}, u32[]{:S(2)}, u32[]{:S(2)}) collective-permute-start(f32[64,128]{1,0:T(8,128)S(1)} %get-tuple-element.26), channel_id=1, source_target_pairs={{0,1},{1,0},{2,3},{3,2},{4,5},{5,4},{6,7},{7,6},{8,9},{9,8},{10,11... | collective-permute-start | bytes 98312 | tf_op jit(solution)/shard_map/ppermute | solution.py:536
  35.3 5.0 %collective-permute-start.3 = (f32[64,128]{1,0:T(8,128)S(1)}, f32[64,128]{1,0:T(8,128)S(1)}, u32[]{:S(2)}, u32[]{:S(2)}) collective-permute-start(f32[64,128]{1,0:T(8,128)S(1)} %add.3.refs_0_), channel_id=1, source_target_pairs={{0,2},{1,3},{2,0},{3,1},{4,6},{5,7},{6,4},{7,5},{8,10},{9,11},{10,... | collective-permute-start | bytes 98312 | tf_op jit(solution)/shard_map/ppermute | solution.py:536
  36.5 4.8 %collective-permute-start.4 = (f32[64,128]{1,0:T(8,128)S(1)}, f32[64,128]{1,0:T(8,128)S(1)}, u32[]{:S(2)}, u32[]{:S(2)}) collective-permute-start(f32[64,128]{1,0:T(8,128)S(1)} %add.3.refs_0_), channel_id=1, source_target_pairs={{0,4},{1,5},{2,6},{3,7},{4,0},{5,1},{6,2},{7,3},{8,12},{9,13},{10,... | collective-permute-start | bytes 98312 | tf_op jit(solution)/shard_map/ppermute | solution.py:536
  38.4 5.7 %collective-permute-start.5 = (f32[64,128]{1,0:T(8,128)S(1)}, f32[64,128]{1,0:T(8,128)S(1)}, u32[]{:S(2)}, u32[]{:S(2)}) collective-permute-start(f32[64,128]{1,0:T(8,128)S(1)} %add.3.refs_0_), channel_id=1, source_target_pairs={{0,6},{1,7},{2,4},{3,5},{4,2},{5,3},{6,0},{7,1},{8,14},{9,15},{10,... | collective-permute-start | bytes 98312 | tf_op jit(solution)/shard_map/ppermute | solution.py:536

commit v4 on v3

--- a/solution.py
+++ b/solution.py
@@ -13,6 +13,7 @@
 LANES = 128
 SLOTS = 32
 TAIL = 32
+INSIDE = "promise_in_bounds"
 
 gauss_sigmas = (0.7, 1.5, 3.0)
 poly_degrees = (4, 2, 2)
@@ -336,15 +337,21 @@
     row8 = iota((8, LANES), 0)
 
     def column(value, at):
-        return jnp.broadcast_to(value[:, at : at + 1], (8, LANES))
+        return jnp.take_along_axis(value, jnp.full((8, LANES), at, jnp.int32), axis=1, mode=INSIDE)
 
     def added(terms):
         while len(terms) > 1:
             terms = [sum(terms[n + 1 : n + 2], terms[n]) for n in range(0, len(terms), 2)]
         return terms[0]
 
+    def column_far(value, at):
+        return jnp.broadcast_to(value[:, at : at + 1], (8, LANES))
+
+    def row_far(value, at):
+        return jnp.broadcast_to(value[at : at + 1, :], (8, LANES))
+
     def row_of(value, at):
-        return jnp.broadcast_to(value[at : at + 1, :], (8, LANES))
+        return jnp.take_along_axis(value, jnp.full((8, LANES), at, jnp.int32), axis=0, mode=INSIDE)
 
     per = SLOTS // 8
     for q in range(NQ):
@@ -354,33 +361,43 @@
             first = 8 * block % LANES
             count = min(8, SCI - 8 * block % SLOTS)
             panel = [column(groups[block][side], first + j) for j in range(count)] + groups[block][side:]
+            known = None
             for k in range(0, count, 2):
                 one, two = panel[k], panel[k + 1]
-                a, b = row_of(one, k), row_of(two, k)
-                c, d = row_of(one, k + 1), row_of(two, k + 1)
+                if known is None:
+                    known = [row_of(x, i) for i in (k, k + 1) for x in (one, two)]
+                a, b, c, d = known
                 inverse = 1.0 / (a * d - b * c)
+                pairs = [(row_of(x, k), row_of(x, k + 1)) for x in panel]
+                first_rest, second_rest = two * c - one * d, one * b - two * a
+                if k + 2 < count:
+                    known = []
+                    for i in (k + 2, k + 3):
+                        before, after = row_of(one, i), row_of(two, i)
+                        first_here, second_here = after * c - before * d, before * b - after * a
+                        for j in (k + 2, k + 3):
+                            step = first_here * pairs[j][0] + second_here * pairs[j][1]
+                            known.append(row_of(panel[j], i) + inverse * step)
                 here, after = row8 == k, row8 == k + 1
-                first_factor = inverse * jnp.where(here, d, jnp.where(after, -c, two * c - one * d))
-                second_factor = inverse * jnp.where(here, -b, jnp.where(after, a, one * b - two * a))
+                first_factor = inverse * jnp.where(here, d, jnp.where(after, -c, first_rest))
+                second_factor = inverse * jnp.where(here, -b, jnp.where(after, a, second_rest))
                 for j in range(k + 2, len(panel)):
                     old = jnp.where(here | after, 0.0, panel[j])
-                    panel[j] = old + (
-                        first_factor * row_of(panel[j], k) + second_factor * row_of(panel[j], k + 1)
-                    )
+                    panel[j] = old + (first_factor * pairs[j][0] + second_factor * pairs[j][1])
             ready = panel[count:]
-            spread_rows = [[row_of(tile, j) for j in range(count)] for tile in ready]
+            spread_rows = [[row_far(tile, j) for j in range(count)] for tile in ready]
             groups[block][side:] = ready
             for i in inner:
                 if i != block:
-                    factors = [column(groups[i][side], first + j) for j in range(count)]
+                    factors = [column_far(groups[i][side], first + j) for j in range(count)]
                     for t in range(side, 2):
                         products = [factors[j] * spread_rows[t - side][j] for j in range(count)]
                         groups[i][t] = groups[i][t] - added(products)
         ahead = list(range((q + 1) * per, (q + 2) * per)) if q + 1 < NQ else []
         for i in ahead:
-            factors = [column(groups[i][side], start + j) for j in range(SCI)]
+            factors = [column_far(groups[i][side], start + j) for j in range(SCI)]
             for t in range(side, 2):
-                products = [factors[j] * row_of(groups[inner[j // 8]][t], j % 8) for j in range(SCI)]
+                products = [factors[j] * row_far(groups[inner[j // 8]][t], j % 8) for j in range(SCI)]
                 groups[i][t] = groups[i][t] - added(products)
         rest = [i for i in range(len(groups)) if i not in inner and i not in ahead]
         left = jnp.concatenate([groups[i][side] for i in rest], axis=0)

time: 51.6 us -> 49.8 us (0.965)
  Pallas kernels: 15.3 us -> 13.5 us
    pallas_call x1, Pallas kernels: 7.15 us -> 5.35 us  [body(): pl.pallas_call(solve_kernel, out_shape=jax.ShapeDtypeStruct((rows, cols),...]
where the time goes in v4:
time: 49.8 us; the launch traced here: 49.4 us
  starting transfers between devices  18.3 us (37%)
  waiting for transfers between devices  16.3 us (33%)
  Pallas kernels  13.5 us (27%)
  between operations  1.36 us (3%)
    ppermute x4, starting transfers between devices, exchanged(): lax.ppermute(value, 'strip', [(i, i ^ step) for i in range(strip_count)])  9.24 us
    all_to_all x1, waiting for transfers between devices, body(): lax.all_to_all(outgoing, ('ccd', 'strip'), split_axis=0, concat_axis=0, t...  8.4 us
    all_to_all x1, starting transfers between devices, body(): lax.all_to_all(outgoing, ('ccd', 'strip'), split_axis=0, concat_axis=0, t...  7.3 us
    ppermute x4, waiting for transfers between devices, exchanged(): lax.ppermute(value, 'strip', [(i, i ^ step) for i in range(strip_count)])  5.58 us
    pallas_call x1, Pallas kernels, body(): pl.pallas_call(solve_kernel, out_shape=jax.ShapeDtypeStruct((rows, cols),...  5.35 us
    pallas_call x1, Pallas kernels, body(): pl.pallas_call(basis_kernel, out_shape=(pltpu.VMEM((rows * SLOTS, cols),...  3.96 us
    ppermute x2, waiting for transfers between devices, swap(): return lax.ppermute(value, 'strip', pairs + [(j, i) for i, j in pairs])  2.33 us
    pallas_call x1, Pallas kernels, body(): pl.pallas_call(pack_kernel, out_shape=jax.ShapeDtypeStruct((device_count,...  1.81 us
  transfers between devices with their start and end apart: 7, of which 5 were waited for; matrix products, arithmetic and copies ran while one was open for 0% of the time, Pallas kernels for 4%

profile of v4, /device:TPU:0, one launch (start us, length us, event | category | flops | bytes accessed | tf_op | source)
XLA Modules:
  0.0 49.4 jit_solution(16201101126731682916)
XLA Ops:
  0.0 1.8 %pack.1 = f32[32,16,128]{2,1,0:T(8,128)} custom-call(f32[18,16,128]{2,1,0:T(8,128)} %store_hbm_ref.1, s32[18,32]{1,0:T(8,128)} %bitcast.3, s32[18,32]{1,0:T(8,128)} %bitcast.2), custom_call_target="tpu_custom_call" | custom-call | tf_op jit(solution)/shard_map/pack/pallas_call | solution.py:470
  1.8 7.3 %all-to-all-start = ((f32[32,16,128]{2,1,0:T(8,128)}), f32[32,16,128]{2,1,0:T(8,128)S(1)}, u32[]{:S(2)}, u32[]{:S(2)}) async-start(f32[32,16,128]{2,1,0:T(8,128)} %pack.1), calls=%async_computation | async-start | bytes 524288 | tf_op jit(solution)/shard_map/all_to_all | solution.py:484
  9.8 1.6 %tables.1 = (s32[18,128]{1,0:T(8,128)S(1)}, bf16[512,1408]{1,0:T(8,128)(2,1)S(1)}, bf16[256,200]{1,0:T(8,128)(2,1)S(1)}, bf16[256,240]{1,0:T(8,128)(2,1)S(1)}) custom-call(s32[18,32]{1,0:T(8,128)} %bitcast.4), custom_call_target="tpu_custom_call" | custom-call | flops 10000000 | bytes 2000000 | tf_op jit(solution)/shard_map/tables/pallas_call | solution.py:485
  11.4 8.4 %all-to-all-done.arrived_ref = f32[32,16,128]{2,1,0:T(8,128)S(1)} async-done(((f32[32,16,128]{2,1,0:T(8,128)}), f32[32,16,128]{2,1,0:T(8,128)S(1)}, u32[]{:S(2)}, u32[]{:S(2)}) %all-to-all-start) | async-done | bytes 262176 | tf_op jit(solution)/shard_map/all_to_all | solution.py:484
  19.8 0.1 window.1
  19.9 1.1 %collective-permute-start = (f32[192,128]{1,0:T(8,128)S(1)}, f32[192,128]{1,0:T(8,128)S(1)}, u32[]{:S(2)}, u32[]{:S(2)}) collective-permute-start(f32[192,128]{1,0:T(8,128)S(1)} %get-tuple-element.21), channel_id=1, source_target_pairs={{0,1},{2,3},{4,5},{6,7},{1,0},{3,2},{5,4},{7,6},{8,9},{10,11},{12,... | collective-permute-start | bytes 294920 | tf_op jit(solution)/shard_map/ppermute | solution.py:515
  21.0 0.7 %collective-permute-start.1 = (f32[192,128]{1,0:T(8,128)S(1)}, f32[192,128]{1,0:T(8,128)S(1)}, u32[]{:S(2)}, u32[]{:S(2)}) collective-permute-start(f32[192,128]{1,0:T(8,128)S(1)} %get-tuple-element.22), channel_id=1, source_target_pairs={{1,2},{3,4},{5,6},{2,1},{4,3},{6,5},{9,10},{11,12},{13,14},{10,9},... | collective-permute-start | bytes 294920 | tf_op jit(solution)/shard_map/ppermute | solution.py:515
  21.7 0.6 %own.1 = (bf16[80,2048]{1,0:T(8,128)(2,1)S(1)}, bf16[96,2048]{1,0:T(8,128)(2,1)S(1)}) custom-call(f32[16,2176]{1,0:T(8,128)S(1)} %get-tuple-element.17.window_ref, bf16[512,1408]{1,0:T(8,128)(2,1)S(1)} %get-tuple-element.18.band_ref), custom_call_target="tpu_custom_call" | custom-call | flops 600000000 | bytes 3000000 | tf_op jit(solution)/shard_map/own/pallas_call | solution.py:520
  22.3 2.3 %collective-permute-done.partner_ref = f32[192,128]{1,0:T(8,128)S(1)} collective-permute-done((f32[192,128]{1,0:T(8,128)S(1)}, f32[192,128]{1,0:T(8,128)S(1)}, u32[]{:S(2)}, u32[]{:S(2)}) %collective-permute-start) | collective-permute-done | bytes 98336 | tf_op jit(solution)/shard_map/ppermute | solution.py:515
  24.6 0.0 collective-permute-done.1.other_ref
  24.6 4.0 %basis.1 = (bf16[512,2048]{1,0:T(8,128)(2,1)S(1)}, f32[64,128]{1,0:T(8,128)S(1)}) custom-call(bf16[80,2048]{1,0:T(8,128)(2,1)S(1)} %get-tuple-element.19.first_own_ref, bf16[96,2048]{1,0:T(8,128)(2,1)S(1)} %get-tuple-element.20.second_own_ref, f32[192,128]{1,0:T(8,128)S(1)} %collective-permute-done.partner_ref, ...), custom_call_target="tpu_custom_call" | custom-call | tf_op jit(solution)/shard_map/basis/pallas_call | solution.py:532
  28.6 4.9 %collective-permute-start.2 = (f32[64,128]{1,0:T(8,128)S(1)}, f32[64,128]{1,0:T(8,128)S(1)}, u32[]{:S(2)}, u32[]{:S(2)}) collective-permute-start(f32[64,128]{1,0:T(8,128)S(1)} %get-tuple-element.26), channel_id=1, source_target_pairs={{0,1},{1,0},{2,3},{3,2},{4,5},{5,4},{6,7},{7,6},{8,9},{9,8},{10,11... | collective-permute-start | bytes 98312 | tf_op jit(solution)/shard_map/ppermute | solution.py:553
  33.4 1.9 %collective-permute-done.2 = f32[64,128]{1,0:T(8,128)S(1)} collective-permute-done((f32[64,128]{1,0:T(8,128)S(1)}, f32[64,128]{1,0:T(8,128)S(1)}, u32[]{:S(2)}, u32[]{:S(2)}) %collective-permute-start.2) | collective-permute-done | bytes 32800 | tf_op jit(solution)/shard_map/ppermute | solution.py:553
  35.3 1.2 %collective-permute-start.3 = (f32[64,128]{1,0:T(8,128)S(1)}, f32[64,128]{1,0:T(8,128)S(1)}, u32[]{:S(2)}, u32[]{:S(2)}) collective-permute-start(f32[64,128]{1,0:T(8,128)S(1)} %add.3.refs_0_), channel_id=1, source_target_pairs={{0,2},{1,3},{2,0},{3,1},{4,6},{5,7},{6,4},{7,5},{8,10},{9,11},{10,... | collective-permute-start | bytes 98312 | tf_op jit(solution)/shard_map/ppermute | solution.py:553
  36.5 1.9 %collective-permute-start.4 = (f32[64,128]{1,0:T(8,128)S(1)}, f32[64,128]{1,0:T(8,128)S(1)}, u32[]{:S(2)}, u32[]{:S(2)}) collective-permute-start(f32[64,128]{1,0:T(8,128)S(1)} %add.3.refs_0_), channel_id=1, source_target_pairs={{0,4},{1,5},{2,6},{3,7},{4,0},{5,1},{6,2},{7,3},{8,12},{9,13},{10,... | collective-permute-start | bytes 98312 | tf_op jit(solution)/shard_map/ppermute | solution.py:553
  38.4 1.4 %collective-permute-start.5 = (f32[64,128]{1,0:T(8,128)S(1)}, f32[64,128]{1,0:T(8,128)S(1)}, u32[]{:S(2)}, u32[]{:S(2)}) collective-permute-start(f32[64,128]{1,0:T(8,128)S(1)} %add.3.refs_0_), channel_id=1, source_target_pairs={{0,6},{1,7},{2,4},{3,5},{4,2},{5,3},{6,0},{7,1},{8,14},{9,15},{10,... | collective-permute-start | bytes 98312 | tf_op jit(solution)/shard_map/ppermute | solution.py:553
  40.4 0.0 collective-permute-done.3.refs_1_
  40.4 0.9 %collective-permute-done.4.refs_2_ = f32[64,128]{1,0:T(8,128)S(1)} collective-permute-done((f32[64,128]{1,0:T(8,128)S(1)}, f32[64,128]{1,0:T(8,128)S(1)}, u32[]{:S(2)}, u32[]{:S(2)}) %collective-permute-start.4) | collective-permute-done | bytes 32800 | tf_op jit(solution)/shard_map/ppermute | solution.py:553
  41.3 2.7 %collective-permute-done.5.refs_3_ = f32[64,128]{1,0:T(8,128)S(1)} collective-permute-done((f32[64,128]{1,0:T(8,128)S(1)}, f32[64,128]{1,0:T(8,128)S(1)}, u32[]{:S(2)}, u32[]{:S(2)}) %collective-permute-start.5) | collective-permute-done | bytes 32800 | tf_op jit(solution)/shard_map/ppermute | solution.py:553
  44.1 5.4 %solve.1 = f32[16,2048]{1,0:T(8,128)} custom-call(s32[1]{0:T(128)S(6)} %copy.8.order_ref, f32[16,2048]{1,0:T(8,128)} %science_hbm_ref.3, bf16[512,2048]{1,0:T(8,128)(2,1)S(1)} %get-tuple-element.25.basis_ref, f32[64,128]{1,0:T(8,128)S(1)} %add.3.refs_0_, f32[64,128]{1,0:T(8,128)S(1)} %collective-permute-done.3.refs_1_, ...), custom_call_target="tpu_custom_call" | custom-call | tf_op jit(solution)/shard_map/solve/pallas_call | solution.py:558
  (1 shorter events, 0.0 us)
Async XLA Ops:
  1.8 18.0 %all-to-all-start = ((f32[32,16,128]{2,1,0:T(8,128)}), f32[32,16,128]{2,1,0:T(8,128)S(1)}, u32[]{:S(2)}, u32[]{:S(2)}) async-start(f32[32,16,128]{2,1,0:T(8,128)} %pack.1), calls=%async_computation | async-start | bytes 524288 | tf_op jit(solution)/shard_map/all_to_all | solution.py:484
  19.9 4.7 %collective-permute-start = (f32[192,128]{1,0:T(8,128)S(1)}, f32[192,128]{1,0:T(8,128)S(1)}, u32[]{:S(2)}, u32[]{:S(2)}) collective-permute-start(f32[192,128]{1,0:T(8,128)S(1)} %get-tuple-element.21), channel_id=1, source_target_pairs={{0,1},{2,3},{4,5},{6,7},{1,0},{3,2},{5,4},{7,6},{8,9},{10,11},{12,... | collective-permute-start | bytes 294920 | tf_op jit(solution)/shard_map/ppermute | solution.py:515
  21.0 3.6 %collective-permute-start.1 = (f32[192,128]{1,0:T(8,128)S(1)}, f32[192,128]{1,0:T(8,128)S(1)}, u32[]{:S(2)}, u32[]{:S(2)}) collective-permute-start(f32[192,128]{1,0:T(8,128)S(1)} %get-tuple-element.22), channel_id=1, source_target_pairs={{1,2},{3,4},{5,6},{2,1},{4,3},{6,5},{9,10},{11,12},{13,14},{10,9},... | collective-permute-start | bytes 294920 | tf_op jit(solution)/shard_map/ppermute | solution.py:515
  28.6 6.8 %collective-permute-start.2 = (f32[64,128]{1,0:T(8,128)S(1)}, f32[64,128]{1,0:T(8,128)S(1)}, u32[]{:S(2)}, u32[]{:S(2)}) collective-permute-start(f32[64,128]{1,0:T(8,128)S(1)} %get-tuple-element.26), channel_id=1, source_target_pairs={{0,1},{1,0},{2,3},{3,2},{4,5},{5,4},{6,7},{7,6},{8,9},{9,8},{10,11... | collective-permute-start | bytes 98312 | tf_op jit(solution)/shard_map/ppermute | solution.py:553
  35.3 5.0 %collective-permute-start.3 = (f32[64,128]{1,0:T(8,128)S(1)}, f32[64,128]{1,0:T(8,128)S(1)}, u32[]{:S(2)}, u32[]{:S(2)}) collective-permute-start(f32[64,128]{1,0:T(8,128)S(1)} %add.3.refs_0_), channel_id=1, source_target_pairs={{0,2},{1,3},{2,0},{3,1},{4,6},{5,7},{6,4},{7,5},{8,10},{9,11},{10,... | collective-permute-start | bytes 98312 | tf_op jit(solution)/shard_map/ppermute | solution.py:553
  36.5 4.8 %collective-permute-start.4 = (f32[64,128]{1,0:T(8,128)S(1)}, f32[64,128]{1,0:T(8,128)S(1)}, u32[]{:S(2)}, u32[]{:S(2)}) collective-permute-start(f32[64,128]{1,0:T(8,128)S(1)} %add.3.refs_0_), channel_id=1, source_target_pairs={{0,4},{1,5},{2,6},{3,7},{4,0},{5,1},{6,2},{7,3},{8,12},{9,13},{10,... | collective-permute-start | bytes 98312 | tf_op jit(solution)/shard_map/ppermute | solution.py:553
  38.4 5.7 %collective-permute-start.5 = (f32[64,128]{1,0:T(8,128)S(1)}, f32[64,128]{1,0:T(8,128)S(1)}, u32[]{:S(2)}, u32[]{:S(2)}) collective-permute-start(f32[64,128]{1,0:T(8,128)S(1)} %add.3.refs_0_), channel_id=1, source_target_pairs={{0,6},{1,7},{2,4},{3,5},{4,2},{5,3},{6,0},{7,1},{8,14},{9,15},{10,... | collective-permute-start | bytes 98312 | tf_op jit(solution)/shard_map/ppermute | solution.py:553

commit v5 on v4

--- a/solution.py
+++ b/solution.py
@@ -91,7 +91,12 @@
     other_ref[count * H :, :] = jnp.zeros((spare, LANES), jnp.float32)
 
 
-def table_kernel(source_ref, owner_ref, band_ref, *vertical_refs, rows, halo):
+def table_kernel(source_ref, science_hbm_ref, owner_ref, science_ref, band_ref, *refs):
+    *vertical_refs, sem = refs
+    rows = science_ref.shape[0]
+    science_copy = pltpu.make_async_copy(science_hbm_ref, science_ref, sem)
+    science_copy.start()
+    even = lax.rem(lax.axis_index("strip"), 2) == 0
     me = lax.axis_index("ccd") * lax.axis_size("strip") + lax.axis_index("strip")
     source = source_ref[...]
     owner = jnp.sum(jnp.where(iota(source.shape, 1) == me, source, 0), axis=1, keepdims=True)
@@ -130,13 +135,12 @@
             scale = jnp.where(here, 1.0 / gauss_sigmas[g], scale)
             weight = jnp.where(here, 1.0 / envelope_norm(gauss_sigmas[g]), weight)
         edge = len(members) * rows
-        own = column - wanted * rows
-        outside = column - edge - wanted * halo
-        is_own = (own >= 0) & (own < rows) & (column < edge)
-        is_above = (outside >= 0) & (outside < H)
-        is_below = (outside >= H) & (outside < 2 * H)
-        row_in = jnp.where(is_own, own + H, jnp.where(is_below, outside + rows, outside))
-        matched = (is_own | ((column >= edge) & (is_above | is_below))) & (wanted >= 0)
+        section = jnp.where(column < edge, 0, jnp.where(column < 2 * edge, 1, 2))
+        local = column - section * edge - wanted * rows
+        is_own = section == 0
+        matched = (local >= 0) & (local < jnp.where(is_own, rows, H)) & (wanted >= 0)
+        is_below = (section == 1) == even
+        row_in = local + jnp.where(is_own, H, jnp.where(is_below, H + rows, 0))
         for r in range(rows):
             a = row_in - (r + H)
             z = a.astype(jnp.float32) * scale
@@ -146,6 +150,7 @@
             power = jnp.where(degree == 3, square * z, jnp.where(degree == 4, square * square, power))
             keep = matched & (jnp.abs(a) <= H)
             vertical_ref[r * HALF : (r + 1) * HALF, :] = jnp.where(keep, tap * power, 0.0).astype(jnp.bfloat16)
+    science_copy.wait()
 
 
 def wide_tile(value):
@@ -197,51 +202,44 @@
     filter_rows(window_ref[...], band_ref, refs[-1], refs[:-1])
 
 
-def basis_kernel(
-    first_own_ref, second_own_ref, partner_ref, other_ref, science_hbm_ref, band_ref, first_ref, second_ref,
-    basis_ref, moment_ref,
-    padded_ref, filtered_ref, first_outside_ref, second_outside_ref, science_ref, sems,
-):
+def row_split(rows):
+    even = lax.rem(lax.axis_index("strip"), 2) == 0
+    return (jnp.where(even, H, 0), rows - H), (jnp.where(even, 0, rows - H), H)
+
+
+def filter_halo(halo_ref, band_ref, padded_ref, filtered_ref, out_refs):
+    rows = padded_ref.shape[0]
+    padded_ref[H:, :] = jnp.zeros((rows - H, padded_ref.shape[1]), jnp.float32)
+    for w in range(padded_ref.shape[1] // LANES):
+        padded_ref[0:H, w * LANES : (w + 1) * LANES] = halo_ref[w * H : (w + 1) * H, :]
+    filter_rows(padded_ref[...], band_ref, filtered_ref, out_refs)
+
+
+def images_and_moments(start, count, vertical_refs, source_refs, science_ref, basis_ref):
     strip_count = lax.axis_size("strip")
     strip = lax.axis_index("strip")
     rows, cols = science_ref.shape
-    blocks = cols // LANES
-    science_copy = pltpu.make_async_copy(science_hbm_ref, science_ref, sems.at[0])
-    science_copy.start()
-    even = lax.rem(strip, 2) == 0
-    padded_ref[2 * H :, :] = jnp.zeros((padded_ref.shape[0] - 2 * H, padded_ref.shape[1]), jnp.float32)
-    for w in range(blocks + 1):
-        at = slice(w * LANES, (w + 1) * LANES)
-        partner, other = partner_ref[w * H : (w + 1) * H, :], other_ref[w * H : (w + 1) * H, :]
-        padded_ref[0:H, at] = jnp.where(even, other, partner)
-        padded_ref[H : 2 * H, at] = jnp.where(even, partner, other)
-    filter_rows(padded_ref[...], band_ref, filtered_ref, (first_outside_ref, second_outside_ref))
-
     eighth = iota((8, 2 * LANES), 0)
-    science_copy.wait()
-    for pair in range(blocks // 2):
+    for pair in range(cols // LANES // 2):
         at = slice(pair * 2 * LANES, (pair + 1) * 2 * LANES)
-        one, two = (
-            jnp.dot(
-                vertical_ref[...],
-                jnp.concatenate([own_ref[:, at], outside_ref[:, at]], axis=0),
-                preferred_element_type=jnp.float32,
-            )
-            for vertical_ref, own_ref, outside_ref in (
-                (first_ref, first_own_ref, first_outside_ref),
-                (second_ref, second_own_ref, second_outside_ref),
-            )
-        )
+        blocks = []
+        for n, vertical_ref in enumerate(vertical_refs):
+            right = jnp.concatenate([refs[n][:, at] for refs in source_refs], axis=0)
+            left = vertical_ref[pl.ds(pl.multiple_of(start * HALF, HALF), count * HALF), 0 : right.shape[0]]
+            blocks.append(jnp.dot(left, right, preferred_element_type=jnp.float32))
+        one, two = blocks
         parts = []
-        for r in range(rows):
+        for r in range(count):
             low, high = r * HALF, (r + 1) * HALF
+            science = science_ref[pl.ds(start + r, 1), at]
             parts += [one[low : high - 8], jnp.where(eighth == ONE % 8, 1.0, one[high - 8 : high])]
-            parts += [two[low : high - 8], jnp.where(eighth == SCI % 8, science_ref[r : r + 1, at], two[high - 8 : high])]
+            parts += [two[low : high - 8], jnp.where(eighth == SCI % 8, science, two[high - 8 : high])]
         basis_ref[:, at] = jnp.concatenate(parts, axis=0).astype(jnp.bfloat16)
+
     u = u_row(cols)
     square = u * u
     totals = [None] * 5
-    for r in range(rows):
+    for r in range(count):
         here = basis_ref[r * SLOTS : (r + 1) * SLOTS, :]
         wide = here.astype(jnp.float32)
         once, twice = (wide * u).astype(jnp.bfloat16), (wide * square).astype(jnp.bfloat16)
@@ -251,37 +249,59 @@
             (((1,), (1,)), ((), ())),
             preferred_element_type=jnp.float32,
         )
-        v = 2.0 * ((strip * rows + r).astype(jnp.float32) + 0.5) / (rows * strip_count) - 1.0
+        v = 2.0 * ((strip * rows + start + r).astype(jnp.float32) + 0.5) / (rows * strip_count) - 1.0
         for c in range(5):
             totals[c] = product if totals[c] is None else totals[c] + product
             product = product * v
-    half = SLOTS // 2
-    row = iota((half, LANES), 0)
-    lane = iota((half, LANES), 1)
-    chunks = [jnp.zeros((half, LANES), jnp.float32) for _ in range(moment_ref.shape[0] // half)]
+    row = iota((HALF, LANES), 0)
+    lane = iota((HALF, LANES), 1)
+    chunks = [jnp.zeros((HALF, LANES), jnp.float32) for _ in range(-(-len(moment_keys) // 4))]
     for at, (a, c) in enumerate(moment_keys):
         first, second = (a, 0) if a < 3 else (a - 2, 1)
         group = at % 4 * SLOTS
-        top = totals[c][first * SLOTS : first * SLOTS + half, :]
-        bottom = totals[c][first * SLOTS + half : (first + 1) * SLOTS, :]
+        top = totals[c][first * SLOTS : first * SLOTS + HALF, :]
+        bottom = totals[c][first * SLOTS + HALF : (first + 1) * SLOTS, :]
         by = group - second * SLOTS
-        corner = jnp.where(lane - group - half <= row, turn_lanes(top, by + half), turn_lanes(bottom, by + 1))
-        both = jnp.where(lane - group < half, turn_lanes(bottom, by), corner)
+        corner = jnp.where(lane - group - HALF <= row, turn_lanes(top, by + HALF), turn_lanes(bottom, by + 1))
+        both = jnp.where(lane - group < HALF, turn_lanes(bottom, by), corner)
         chunks[at // 4] = jnp.where(lane // SLOTS == at % 4, both, chunks[at // 4])
-    for p, chunk in enumerate(chunks):
-        moment_ref[p * half : (p + 1) * half, :] = chunk
-
-
-def solve_kernel(order_ref, science_hbm_ref, basis_ref, *refs):
-    out_hbm_ref, system_ref, science_ref, out_ref, sem, sems = refs[-6:]
+    return jnp.concatenate(chunks, axis=0)
+
+
+def early_kernel(
+    first_own_ref, second_own_ref, partner_ref, science_ref, band_ref, first_ref, second_ref,
+    basis_ref, moment_ref, first_partner_ref, second_partner_ref,
+    padded_ref, filtered_ref,
+):
+    partner_refs = first_partner_ref, second_partner_ref
+    filter_halo(partner_ref, band_ref, padded_ref, filtered_ref, partner_refs)
+    start, count = row_split(science_ref.shape[0])[0]
+    sources = (first_own_ref, second_own_ref), partner_refs
+    moment_ref[...] = images_and_moments(start, count, (first_ref, second_ref), sources, science_ref, basis_ref)
+
+
+def late_kernel(
+    first_own_ref, second_own_ref, first_partner_ref, second_partner_ref, other_ref, early_ref,
+    science_ref, band_ref, first_ref, second_ref,
+    basis_ref, moment_ref,
+    padded_ref, filtered_ref, first_other_ref, second_other_ref,
+):
+    other_refs = first_other_ref, second_other_ref
+    filter_halo(other_ref, band_ref, padded_ref, filtered_ref, other_refs)
+    start, count = row_split(science_ref.shape[0])[1]
+    sources = (first_own_ref, second_own_ref), (first_partner_ref, second_partner_ref), other_refs
+    moments = images_and_moments(start, count, (first_ref, second_ref), sources, science_ref, basis_ref)
+    moment_ref[...] = early_ref[...] + moments
+
+
+def solve_kernel(order_ref, science_ref, early_ref, late_ref, *refs):
+    out_hbm_ref, system_ref, out_ref, sems = refs[-4:]
     strip_count = lax.axis_size("strip")
     strip = lax.axis_index("strip")
     rows, cols = science_ref.shape
-    copy = pltpu.make_async_copy(science_hbm_ref, science_ref, sem)
-    copy.start()
     order = order_ref[0]
     total = refs[0][...]
-    for ref in refs[1:-6]:
+    for ref in refs[1:-4]:
         total = total + ref[...]
     half = SLOTS // 2
     across = jnp.transpose(jnp.concatenate([total, jnp.zeros((LANES - total.shape[0], LANES), jnp.float32)], axis=0))
@@ -420,25 +440,24 @@
     weights = [jnp.zeros((rows, LANES), jnp.float32) for _ in range(3)]
     for q, (a, c) in enumerate(mono_powers):
         weights[a] = weights[a] + turned[q] * (v * v if c == 2 else v if c else jnp.ones_like(v))
-    spread = jnp.concatenate(
-        [
-            jnp.concatenate(
-                [jnp.where(group + m * (LANES // SLOTS) == row, w, 0.0) for m in range(rows * SLOTS // LANES)],
-                axis=1,
-            )
-            for w in weights
-        ],
-        axis=0,
-    )
-    spread_high, spread_low = split_two(spread)
-    spread = jnp.concatenate([spread_high, spread_low], axis=0)
-    copy.wait()
+    def spread(start, count):
+        pieces = []
+        for weight in weights:
+            tiles = []
+            for m in range(-(-count * SLOTS // LANES)):
+                place = group + m * (LANES // SLOTS)
+                tiles.append(jnp.where((place + start == row) & (place < count), weight, 0.0))
+            pieces.append(jnp.concatenate(tiles, axis=1))
+        high, low = split_two(jnp.concatenate(pieces, axis=0))
+        return jnp.concatenate([high, low], axis=0)[:, : count * SLOTS]
+
+    images = [(spread(*part), ref) for part, ref in zip(row_split(rows), (early_ref, late_ref))]
     u = u_row(cols)
     step = cols // sems.shape[0]
     writes = []
     for n in range(sems.shape[0]):
         at = slice(n * step, (n + 1) * step)
-        sums = jnp.dot(spread, basis_ref[:, at], preferred_element_type=jnp.float32)
+        sums = sum(jnp.dot(x, ref[:, at], preferred_element_type=jnp.float32) for x, ref in images)
         model = [sums[a * rows : (a + 1) * rows] + sums[(a + 3) * rows : (a + 4) * rows] for a in range(3)]
         out_ref[:, at] = science_ref[:, at] - (model[0] + u[:, at] * (model[1] + u[:, at] * model[2]))
         writes.append(pltpu.make_async_copy(out_ref.at[:, at], out_hbm_ref.at[:, at], sems.at[n]))
@@ -451,7 +470,6 @@
     strip_count = lax.axis_size("strip")
     device_count = lax.axis_size("ccd") * strip_count
     rows, cols = science.shape
-    halo = -(-2 * H // 8) * 8
     vmem = pl.BlockSpec(memory_space=pltpu.VMEM)
     smem = pl.BlockSpec(memory_space=pltpu.SMEM)
     hbm = pl.BlockSpec(memory_space=pltpu.HBM)
@@ -482,19 +500,21 @@
         name="pack",
     )(tile_store, source, slot)
     arrived = lax.all_to_all(outgoing, ("ccd", "strip"), split_axis=0, concat_axis=0, tiled=True)
-    owner, band, *vertical = pl.pallas_call(
-        lambda *refs: table_kernel(*refs, rows=rows, halo=halo),
+    owner, science, band, *vertical = pl.pallas_call(
+        table_kernel,
         out_shape=(
             pltpu.VMEM((tile_source.shape[1], LANES), jnp.int32),
+            pltpu.VMEM((rows, cols), jnp.float32),
             pltpu.VMEM((4 * LANES, NF * LANES), jnp.bfloat16),
         )
-        + tuple(pltpu.VMEM((rows * HALF, len(m) * (rows + halo)), jnp.bfloat16) for m in filter_sets),
-        in_specs=[vmem],
-        out_specs=(vmem,) * 4,
+        + tuple(pltpu.VMEM((rows * HALF, 3 * len(m) * rows), jnp.bfloat16) for m in filter_sets),
+        in_specs=[vmem, hbm],
+        out_specs=(vmem,) * 5,
+        scratch_shapes=[pltpu.SemaphoreType.DMA],
         compiler_params=params(16),
         name="tables",
         cost_estimate=pl.CostEstimate(flops=10_000_000, bytes_accessed=2_000_000, transcendentals=1_000_000),
-    )(source)
+    )(source, science)
     count = cols // LANES + 1
     edge = -(-count * H // 8) * 8
     window, to_partner, to_other = pl.pallas_call(
@@ -527,27 +547,41 @@
         name="own",
         cost_estimate=pl.CostEstimate(flops=600_000_000, bytes_accessed=3_000_000, transcendentals=0),
     )(window, kept(band))
-    half = SLOTS // 2
-    packed = -(-len(moment_keys) // 4) * half
-    basis, moments = pl.pallas_call(
-        basis_kernel,
+    packed = -(-len(moment_keys) // 4) * HALF
+    halves = tuple(pltpu.VMEM((len(m) * rows, cols), jnp.bfloat16) for m in filter_sets)
+    (_, early_count), (_, late_count) = row_split(rows)
+    working = [
+        pltpu.VMEM((rows, count * LANES), jnp.float32),
+        pltpu.VMEM((cols // LANES * rows, NF * LANES), jnp.float32),
+    ]
+    science = kept(science)
+    band, filtered_own, vertical = kept(band), [*map(kept, filtered_own)], [*map(kept, vertical)]
+    early, early_moments, *filtered_partner = pl.pallas_call(
+        early_kernel,
         out_shape=(
-            pltpu.VMEM((rows * SLOTS, cols), jnp.bfloat16),
+            pltpu.VMEM((early_count * SLOTS, cols), jnp.bfloat16),
+            pltpu.VMEM((packed, LANES), jnp.float32),
+        )
+        + halves,
+        in_specs=[vmem] * 7,
+        out_specs=(vmem,) * 4,
+        scratch_shapes=working,
+        compiler_params=params(16),
+        name="early",
+        cost_estimate=pl.CostEstimate(flops=1_000_000_000, bytes_accessed=4_000_000, transcendentals=0),
+    )(*filtered_own, from_partner, science, band, *vertical)
+    late, moments = pl.pallas_call(
+        late_kernel,
+        out_shape=(
+            pltpu.VMEM((late_count * SLOTS, cols), jnp.bfloat16),
             pltpu.VMEM((packed, LANES), jnp.float32),
         ),
-        in_specs=[vmem, vmem, vmem, vmem, hbm, vmem, vmem, vmem],
+        in_specs=[vmem] * 10,
         out_specs=(vmem, vmem),
-        scratch_shapes=[
-            pltpu.VMEM((halo, count * LANES), jnp.float32),
-            pltpu.VMEM((cols // LANES * halo, NF * LANES), jnp.float32),
-            pltpu.VMEM((len(filter_sets[0]) * halo, cols), jnp.bfloat16),
-            pltpu.VMEM((len(filter_sets[1]) * halo, cols), jnp.bfloat16),
-            pltpu.VMEM((rows, cols), jnp.float32),
-            pltpu.SemaphoreType.DMA((1,)),
-        ],
+        scratch_shapes=working + [pltpu.VMEM((len(m) * rows, cols), jnp.bfloat16) for m in filter_sets],
         compiler_params=params(24),
-        name="basis",
-    )(*map(kept, filtered_own), from_partner, from_other, science, *map(kept, (band, *vertical)))
+        name="late",
+    )(*filtered_own, *map(kept, filtered_partner), from_other, kept(early_moments), science, band, *vertical)
 
     def exchanged(value, step):
         return lax.ppermute(value, "strip", [(i, i ^ step) for i in range(strip_count)])
@@ -558,18 +592,16 @@
     return pl.pallas_call(
         solve_kernel,
         out_shape=jax.ShapeDtypeStruct((rows, cols), jnp.float32),
-        in_specs=[smem, hbm, vmem] + [vmem] * len(parts),
+        in_specs=[smem, vmem, vmem, vmem] + [vmem] * len(parts),
         out_specs=hbm,
         scratch_shapes=[
             pltpu.VMEM((NQ * SLOTS, 2 * LANES), jnp.float32),
             pltpu.VMEM((rows, cols), jnp.float32),
-            pltpu.VMEM((rows, cols), jnp.float32),
-            pltpu.SemaphoreType.DMA,
             pltpu.SemaphoreType.DMA((4,)),
         ],
         compiler_params=params(16),
         name="solve",
-    )(spatial_order, science, kept(basis), *parts)
+    )(spatial_order, science, kept(early), kept(late), *parts)
 
 
 def solution(mesh):

time: 49.8 us -> 48.7 us (0.978)
  starting transfers between devices: 18.3 us -> 16.7 us
  Pallas kernels: 13.5 us -> 14 us
    ppermute x4, starting transfers between devices: 9.24 us -> 7.63 us  [exchanged(): lax.ppermute(value, 'strip', [(i, i ^ step) for i in range(strip_count)])]
    pallas_call x2 -> x3, Pallas kernels: 5.56 us -> 5.92 us  [the longest x1 2.6 us: body(): pl.pallas_call(late_kernel, out_shape=(pltpu.VMEM((late_count * SLOTS, co...]
  transfers between devices with their start and end apart: 7 -> 7, of which waited for: 5 -> 5; matrix products, arithmetic and copies ran while one was open for 0% -> 0% of each run, Pallas kernels for 4% -> 8%
where the time goes in v5:
time: 48.7 us; the launch traced here: 48.3 us
  starting transfers between devices  16.7 us (34%)
  waiting for transfers between devices  16.2 us (33%)
  Pallas kernels  14 us (29%)
  between operations  1.38 us (3%)
    all_to_all x1, waiting for transfers between devices, body(): lax.all_to_all(outgoing, ('ccd', 'strip'), split_axis=0, concat_axis=0, t...  8.3 us
    ppermute x4, starting transfers between devices, exchanged(): lax.ppermute(value, 'strip', [(i, i ^ step) for i in range(strip_count)])  7.63 us
    all_to_all x1, starting transfers between devices, body(): lax.all_to_all(outgoing, ('ccd', 'strip'), split_axis=0, concat_axis=0, t...  7.3 us
    ppermute x4, waiting for transfers between devices, exchanged(): lax.ppermute(value, 'strip', [(i, i ^ step) for i in range(strip_count)])  5.57 us
    pallas_call x1, Pallas kernels, body(): pl.pallas_call(solve_kernel, out_shape=jax.ShapeDtypeStruct((rows, cols),...  5.56 us
    pallas_call x1, Pallas kernels, body(): pl.pallas_call(late_kernel, out_shape=(pltpu.VMEM((late_count * SLOTS, co...  2.6 us
    ppermute x2, waiting for transfers between devices, swap(): return lax.ppermute(value, 'strip', pairs + [(j, i) for i, j in pairs])  2.35 us
    pallas_call x1, Pallas kernels, body(): pl.pallas_call(pack_kernel, out_shape=jax.ShapeDtypeStruct((device_count,...  1.81 us
  transfers between devices with their start and end apart: 7, of which 5 were waited for; matrix products, arithmetic and copies ran while one was open for 0% of the time, Pallas kernels for 8%

profile of v5, /device:TPU:0, one launch (start us, length us, event | category | flops | bytes accessed | tf_op | source)
XLA Modules:
  0.0 48.3 jit_solution(1469396363518002146)
XLA Ops:
  0.0 1.8 %pack.1 = f32[32,16,128]{2,1,0:T(8,128)} custom-call(f32[18,16,128]{2,1,0:T(8,128)} %store_hbm_ref.1, s32[18,32]{1,0:T(8,128)} %bitcast.3, s32[18,32]{1,0:T(8,128)} %bitcast.2), custom_call_target="tpu_custom_call" | custom-call | tf_op jit(solution)/shard_map/pack/pallas_call | solution.py:488
  1.8 7.3 %all-to-all-start = ((f32[32,16,128]{2,1,0:T(8,128)}), f32[32,16,128]{2,1,0:T(8,128)S(1)}, u32[]{:S(2)}, u32[]{:S(2)}) async-start(f32[32,16,128]{2,1,0:T(8,128)} %pack.1), calls=%async_computation | async-start | bytes 524288 | tf_op jit(solution)/shard_map/all_to_all | solution.py:502
  9.8 1.7 %tables.1 = (s32[18,128]{1,0:T(8,128)S(1)}, f32[16,2048]{1,0:T(8,128)S(1)}, bf16[512,1408]{1,0:T(8,128)(2,1)S(1)}, bf16[256,240]{1,0:T(8,128)(2,1)S(1)}, bf16[256,288]{1,0:T(8,128)(2,1)S(1)}) custom-call(s32[18,32]{1,0:T(8,128)} %bitcast.4, f32[16,2048]{1,0:T(8,128)} %science_hbm_ref.1), custom_call_target="tpu_custom_call" | custom-call | flops 10000000 | bytes 2000000 | tf_op jit(solution)/shard_map/tables/pallas_call | solution.py:503
  11.5 8.3 %all-to-all-done.arrived_ref = f32[32,16,128]{2,1,0:T(8,128)S(1)} async-done(((f32[32,16,128]{2,1,0:T(8,128)}), f32[32,16,128]{2,1,0:T(8,128)S(1)}, u32[]{:S(2)}, u32[]{:S(2)}) %all-to-all-start) | async-done | bytes 262176 | tf_op jit(solution)/shard_map/all_to_all | solution.py:502
  19.8 0.1 window.1
  19.9 1.1 %collective-permute-start = (f32[192,128]{1,0:T(8,128)S(1)}, f32[192,128]{1,0:T(8,128)S(1)}, u32[]{:S(2)}, u32[]{:S(2)}) collective-permute-start(f32[192,128]{1,0:T(8,128)S(1)} %get-tuple-element.27), channel_id=1, source_target_pairs={{0,1},{2,3},{4,5},{6,7},{1,0},{3,2},{5,4},{7,6},{8,9},{10,11},{12,... | collective-permute-start | bytes 294920 | tf_op jit(solution)/shard_map/ppermute | solution.py:535
  21.0 0.7 %collective-permute-start.1 = (f32[192,128]{1,0:T(8,128)S(1)}, f32[192,128]{1,0:T(8,128)S(1)}, u32[]{:S(2)}, u32[]{:S(2)}) collective-permute-start(f32[192,128]{1,0:T(8,128)S(1)} %get-tuple-element.33), channel_id=1, source_target_pairs={{1,2},{3,4},{5,6},{2,1},{4,3},{6,5},{9,10},{11,12},{13,14},{10,9},... | collective-permute-start | bytes 294920 | tf_op jit(solution)/shard_map/ppermute | solution.py:535
  21.7 0.6 %own.1 = (bf16[80,2048]{1,0:T(8,128)(2,1)S(1)}, bf16[96,2048]{1,0:T(8,128)(2,1)S(1)}) custom-call(f32[16,2176]{1,0:T(8,128)S(1)} %get-tuple-element.23.window_ref, bf16[512,1408]{1,0:T(8,128)(2,1)S(1)} %get-tuple-element.24.band_ref), custom_call_target="tpu_custom_call" | custom-call | flops 600000000 | bytes 3000000 | tf_op jit(solution)/shard_map/own/pallas_call | solution.py:540
  22.3 2.3 %collective-permute-done.partner_ref = f32[192,128]{1,0:T(8,128)S(1)} collective-permute-done((f32[192,128]{1,0:T(8,128)S(1)}, f32[192,128]{1,0:T(8,128)S(1)}, u32[]{:S(2)}, u32[]{:S(2)}) %collective-permute-start) | collective-permute-done | bytes 98336 | tf_op jit(solution)/shard_map/ppermute | solution.py:535
  24.6 1.6 %early.1 = (bf16[160,2048]{1,0:T(8,128)(2,1)S(1)}, f32[64,128]{1,0:T(8,128)S(1)}, bf16[80,2048]{1,0:T(8,128)(2,1)S(1)}, bf16[96,2048]{1,0:T(8,128)(2,1)S(1)}) custom-call(bf16[80,2048]{1,0:T(8,128)(2,1)S(1)} %get-tuple-element.25.first_own_ref, bf16[96,2048]{1,0:T(8,128)(2,1)S(1)} %get-tuple-element.26.second_own_ref, ...), custom_call_target="tpu_custom_call" | custom-call | flops 1000000000 | bytes 4000000 | tf_op jit(solution)/shard_map/early/pallas_call | solution.py:559
  26.2 0.0 collective-permute-done.1.other_ref
  26.3 2.6 %late.1 = (bf16[352,2048]{1,0:T(8,128)(2,1)S(1)}, f32[64,128]{1,0:T(8,128)S(1)}) custom-call(bf16[80,2048]{1,0:T(8,128)(2,1)S(1)} %get-tuple-element.25.first_own_ref, bf16[96,2048]{1,0:T(8,128)(2,1)S(1)} %get-tuple-element.26.second_own_ref, bf16[80,2048]{1,0:T(8,128)(2,1)S(1)} %get-tuple-element.31.first_partner_ref, ...), custom_call_target="tpu_custom_call" | custom-call | tf_op jit(solution)/shard_map/late/pallas_call | solution.py:573
  28.9 3.2 %collective-permute-start.2 = (f32[64,128]{1,0:T(8,128)S(1)}, f32[64,128]{1,0:T(8,128)S(1)}, u32[]{:S(2)}, u32[]{:S(2)}) collective-permute-start(f32[64,128]{1,0:T(8,128)S(1)} %get-tuple-element.36), channel_id=1, source_target_pairs={{0,1},{1,0},{2,3},{3,2},{4,5},{5,4},{6,7},{7,6},{8,9},{9,8},{10,11... | collective-permute-start | bytes 98312 | tf_op jit(solution)/shard_map/ppermute | solution.py:587
  32.1 1.9 %collective-permute-done.2 = f32[64,128]{1,0:T(8,128)S(1)} collective-permute-done((f32[64,128]{1,0:T(8,128)S(1)}, f32[64,128]{1,0:T(8,128)S(1)}, u32[]{:S(2)}, u32[]{:S(2)}) %collective-permute-start.2) | collective-permute-done | bytes 32800 | tf_op jit(solution)/shard_map/ppermute | solution.py:587
  34.0 1.2 %collective-permute-start.3 = (f32[64,128]{1,0:T(8,128)S(1)}, f32[64,128]{1,0:T(8,128)S(1)}, u32[]{:S(2)}, u32[]{:S(2)}) collective-permute-start(f32[64,128]{1,0:T(8,128)S(1)} %add.3.refs_0_), channel_id=1, source_target_pairs={{0,2},{1,3},{2,0},{3,1},{4,6},{5,7},{6,4},{7,5},{8,10},{9,11},{10,... | collective-permute-start | bytes 98312 | tf_op jit(solution)/shard_map/ppermute | solution.py:587
  35.2 1.9 %collective-permute-start.4 = (f32[64,128]{1,0:T(8,128)S(1)}, f32[64,128]{1,0:T(8,128)S(1)}, u32[]{:S(2)}, u32[]{:S(2)}) collective-permute-start(f32[64,128]{1,0:T(8,128)S(1)} %add.3.refs_0_), channel_id=1, source_target_pairs={{0,4},{1,5},{2,6},{3,7},{4,0},{5,1},{6,2},{7,3},{8,12},{9,13},{10,... | collective-permute-start | bytes 98312 | tf_op jit(solution)/shard_map/ppermute | solution.py:587
  37.0 1.4 %collective-permute-start.5 = (f32[64,128]{1,0:T(8,128)S(1)}, f32[64,128]{1,0:T(8,128)S(1)}, u32[]{:S(2)}, u32[]{:S(2)}) collective-permute-start(f32[64,128]{1,0:T(8,128)S(1)} %add.3.refs_0_), channel_id=1, source_target_pairs={{0,6},{1,7},{2,4},{3,5},{4,2},{5,3},{6,0},{7,1},{8,14},{9,15},{10,... | collective-permute-start | bytes 98312 | tf_op jit(solution)/shard_map/ppermute | solution.py:587
  39.0 0.0 collective-permute-done.3.refs_1_
  39.1 0.9 %collective-permute-done.4.refs_2_ = f32[64,128]{1,0:T(8,128)S(1)} collective-permute-done((f32[64,128]{1,0:T(8,128)S(1)}, f32[64,128]{1,0:T(8,128)S(1)}, u32[]{:S(2)}, u32[]{:S(2)}) %collective-permute-start.4) | collective-permute-done | bytes 32800 | tf_op jit(solution)/shard_map/ppermute | solution.py:587
  40.0 2.7 %collective-permute-done.5.refs_3_ = f32[64,128]{1,0:T(8,128)S(1)} collective-permute-done((f32[64,128]{1,0:T(8,128)S(1)}, f32[64,128]{1,0:T(8,128)S(1)}, u32[]{:S(2)}, u32[]{:S(2)}) %collective-permute-start.5) | collective-permute-done | bytes 32800 | tf_op jit(solution)/shard_map/ppermute | solution.py:587
  42.7 5.6 %solve.1 = f32[16,2048]{1,0:T(8,128)} custom-call(s32[1]{0:T(128)S(6)} %copy.8.order_ref, f32[16,2048]{1,0:T(8,128)S(1)} %get-tuple-element.21.science_ref, bf16[160,2048]{1,0:T(8,128)(2,1)S(1)} %get-tuple-element.30.early_ref, bf16[352,2048]{1,0:T(8,128)(2,1)S(1)} %get-tuple-element.35.late_ref, f32[64,128]{1,0:T(8,128)S(1)} %add.3.refs_0_, ...), custom_call_target="tpu_custom_call" | custom-call | tf_op jit(solution)/shard_map/solve/pallas_call | solution.py:592
  (1 shorter events, 0.0 us)
Async XLA Ops:
  1.8 18.0 %all-to-all-start = ((f32[32,16,128]{2,1,0:T(8,128)}), f32[32,16,128]{2,1,0:T(8,128)S(1)}, u32[]{:S(2)}, u32[]{:S(2)}) async-start(f32[32,16,128]{2,1,0:T(8,128)} %pack.1), calls=%async_computation | async-start | bytes 524288 | tf_op jit(solution)/shard_map/all_to_all | solution.py:502
  19.9 4.7 %collective-permute-start = (f32[192,128]{1,0:T(8,128)S(1)}, f32[192,128]{1,0:T(8,128)S(1)}, u32[]{:S(2)}, u32[]{:S(2)}) collective-permute-start(f32[192,128]{1,0:T(8,128)S(1)} %get-tuple-element.27), channel_id=1, source_target_pairs={{0,1},{2,3},{4,5},{6,7},{1,0},{3,2},{5,4},{7,6},{8,9},{10,11},{12,... | collective-permute-start | bytes 294920 | tf_op jit(solution)/shard_map/ppermute | solution.py:535
  21.0 5.2 %collective-permute-start.1 = (f32[192,128]{1,0:T(8,128)S(1)}, f32[192,128]{1,0:T(8,128)S(1)}, u32[]{:S(2)}, u32[]{:S(2)}) collective-permute-start(f32[192,128]{1,0:T(8,128)S(1)} %get-tuple-element.33), channel_id=1, source_target_pairs={{1,2},{3,4},{5,6},{2,1},{4,3},{6,5},{9,10},{11,12},{13,14},{10,9},... | collective-permute-start | bytes 294920 | tf_op jit(solution)/shard_map/ppermute | solution.py:535
  28.9 5.1 %collective-permute-start.2 = (f32[64,128]{1,0:T(8,128)S(1)}, f32[64,128]{1,0:T(8,128)S(1)}, u32[]{:S(2)}, u32[]{:S(2)}) collective-permute-start(f32[64,128]{1,0:T(8,128)S(1)} %get-tuple-element.36), channel_id=1, source_target_pairs={{0,1},{1,0},{2,3},{3,2},{4,5},{5,4},{6,7},{7,6},{8,9},{9,8},{10,11... | collective-permute-start | bytes 98312 | tf_op jit(solution)/shard_map/ppermute | solution.py:587
  34.0 5.0 %collective-permute-start.3 = (f32[64,128]{1,0:T(8,128)S(1)}, f32[64,128]{1,0:T(8,128)S(1)}, u32[]{:S(2)}, u32[]{:S(2)}) collective-permute-start(f32[64,128]{1,0:T(8,128)S(1)} %add.3.refs_0_), channel_id=1, source_target_pairs={{0,2},{1,3},{2,0},{3,1},{4,6},{5,7},{6,4},{7,5},{8,10},{9,11},{10,... | collective-permute-start | bytes 98312 | tf_op jit(solution)/shard_map/ppermute | solution.py:587
  35.2 4.8 %collective-permute-start.4 = (f32[64,128]{1,0:T(8,128)S(1)}, f32[64,128]{1,0:T(8,128)S(1)}, u32[]{:S(2)}, u32[]{:S(2)}) collective-permute-start(f32[64,128]{1,0:T(8,128)S(1)} %add.3.refs_0_), channel_id=1, source_target_pairs={{0,4},{1,5},{2,6},{3,7},{4,0},{5,1},{6,2},{7,3},{8,12},{9,13},{10,... | collective-permute-start | bytes 98312 | tf_op jit(solution)/shard_map/ppermute | solution.py:587
  37.0 5.7 %collective-permute-start.5 = (f32[64,128]{1,0:T(8,128)S(1)}, f32[64,128]{1,0:T(8,128)S(1)}, u32[]{:S(2)}, u32[]{:S(2)}) collective-permute-start(f32[64,128]{1,0:T(8,128)S(1)} %add.3.refs_0_), channel_id=1, source_target_pairs={{0,6},{1,7},{2,4},{3,5},{4,2},{5,3},{6,0},{7,1},{8,14},{9,15},{10,... | collective-permute-start | bytes 98312 | tf_op jit(solution)/shard_map/ppermute | solution.py:587
